TPU v7x, 128 devices: a whole 4x4x4 slice. The times are simulated.
128 devices in a mesh: seq: 32 (over y, x, z_lo), col: 4 (over z_hi, core).
Axes of the slice: x: 4, y: 4, z: 4 (z_hi: 2, z_lo: 2; z = z_hi * 2 + z_lo), core: 2. Of those that a mesh axis runs over, the one named last changes fastest.
Arguments:
- q_row: bfloat16 [256, 512, 768], P('seq', 'col'), may hold values from -15 to 15
- k_row: bfloat16 [256, 512, 768], P('seq', 'col'), may hold values from -6 to 6
- v_row: bfloat16 [256, 512, 768], P('seq', 'col'), may hold values from -6 to 6
- q_col: bfloat16 [256, 512, 768], P('seq', 'col'), may hold values from -8 to 8
- k_col: bfloat16 [256, 512, 768], P('seq', 'col'), may hold values from -4 to 4
- out_grad: bfloat16 [256, 512, 768], P('seq', 'col'), may hold values from -6 to 6
Outputs:
- q_row_grad: bfloat16 [256, 512, 768], P('seq', 'col')
- k_row_grad: bfloat16 [256, 512, 768], P('seq', 'col')
- v_row_grad: bfloat16 [256, 512, 768], P('seq', 'col')
- q_col_grad: bfloat16 [256, 512, 768], P('seq', 'col')
- k_col_grad: bfloat16 [256, 512, 768], P('seq', 'col')
All inputs are finite; a program needn't handle non-finite values.
Results may differ from a plain program's by a relative error of at most 0.035.
Values may be sent and summed in bfloat16 or wider, within the bound.
A program may use at most 192 MiB of HBM per device.

v0:
```python
import math

import jax
import jax.numpy as jnp
from jax import lax
from jax.sharding import PartitionSpec as P

DH = 64


def softmax_rows(scores):
    largest = jnp.max(scores, axis=-1, keepdims=True)
    weights = jnp.exp(scores - largest)
    return weights / jnp.sum(weights, axis=-1, keepdims=True)


def slope_rows(probabilities, gradients):
    return probabilities * (gradients - jnp.sum(probabilities * gradients, axis=-1, keepdims=True))


def on_device(q_row, k_row, v_row, q_col, k_col, out_grad):
    row_dev, col_dev, model_width = q_row.shape
    head_count = model_width // DH
    row_total = row_dev * lax.axis_size("seq")
    row_scale = 1.0 / math.sqrt(DH * row_total)
    col_scale = 1.0 / math.sqrt(DH)
    keys_all, values_all = (
        lax.all_gather(k_row, "col", axis=1, tiled=True),
        lax.all_gather(v_row, "col", axis=1, tiled=True),
    )
    col_total = keys_all.shape[1]
    query_heads = q_row.reshape(row_dev, col_dev, head_count, DH)
    key_heads = keys_all.reshape(row_dev, col_total, head_count, DH)
    value_heads = values_all.reshape(row_dev, col_total, head_count, DH)
    partial_logits = jnp.einsum(
        "rihe,rjhe->hij", query_heads, key_heads, preferred_element_type=jnp.float32
    )
    tied = softmax_rows(lax.psum(partial_logits, "seq") * row_scale)
    tied_half = tied.astype(jnp.bfloat16)
    row_output = jnp.einsum(
        "hij,rjhe->rihe", tied_half, value_heads, preferred_element_type=jnp.float32
    )
    row_output = row_output.astype(jnp.bfloat16).reshape(row_dev, col_dev, model_width)
    col_query, col_key, col_cotangent, col_values = (
        lax.all_to_all(q_col, "seq", split_axis=1, concat_axis=0, tiled=True),
        lax.all_to_all(k_col, "seq", split_axis=1, concat_axis=0, tiled=True),
        lax.all_to_all(out_grad, "seq", split_axis=1, concat_axis=0, tiled=True),
        lax.all_to_all(row_output, "seq", split_axis=1, concat_axis=0, tiled=True),
    )
    col_share = col_query.shape[1]
    head_shape = (row_total, col_share, head_count, DH)
    col_query = col_query.reshape(head_shape)
    col_key = col_key.reshape(head_shape)
    col_cotangent = col_cotangent.reshape(head_shape)
    col_values = col_values.reshape(head_shape)
    col_probs = softmax_rows(
        jnp.einsum("rche,sche->chrs", col_query, col_key, preferred_element_type=jnp.float32)
        * col_scale
    )
    col_half = col_probs.astype(jnp.bfloat16)
    col_grads = jnp.einsum(
        "rche,sche->chrs", col_cotangent, col_values, preferred_element_type=jnp.float32
    )
    col_slopes = slope_rows(col_probs, col_grads).astype(jnp.bfloat16)
    flat_shape = (row_total, col_share, model_width)
    mixed_grad = jnp.einsum(
        "chrs,rche->sche", col_half, col_cotangent, preferred_element_type=jnp.float32
    )
    mixed_grad = mixed_grad.astype(jnp.bfloat16).reshape(flat_shape)
    query_col_grad = jnp.einsum(
        "chrs,sche->rche", col_slopes, col_key, preferred_element_type=jnp.float32
    )
    query_col_grad = (query_col_grad * col_scale).astype(jnp.bfloat16).reshape(flat_shape)
    key_col_grad = jnp.einsum(
        "chrs,rche->sche", col_slopes, col_query, preferred_element_type=jnp.float32
    )
    key_col_grad = (key_col_grad * col_scale).astype(jnp.bfloat16).reshape(flat_shape)
    query_col_back, key_col_back, mixed_back = (
        lax.all_to_all(query_col_grad, "seq", split_axis=0, concat_axis=1, tiled=True),
        lax.all_to_all(key_col_grad, "seq", split_axis=0, concat_axis=1, tiled=True),
        lax.all_to_all(mixed_grad, "seq", split_axis=0, concat_axis=1, tiled=True),
    )
    mixed_heads = mixed_back.reshape(row_dev, col_dev, head_count, DH)
    partial_slopes = jnp.einsum(
        "rihe,rjhe->hij", mixed_heads, value_heads, preferred_element_type=jnp.float32
    )
    tied_grads = lax.psum(partial_slopes.astype(jnp.bfloat16), "seq").astype(jnp.float32)
    tied_slopes = slope_rows(tied, tied_grads).astype(jnp.bfloat16)
    query_row_grad = jnp.einsum(
        "hij,rjhe->rihe", tied_slopes, key_heads, preferred_element_type=jnp.float32
    )
    query_row_grad = (
        (query_row_grad * row_scale).astype(jnp.bfloat16).reshape(row_dev, col_dev, model_width)
    )
    key_term = jnp.einsum(
        "hij,rihe->rjhe", tied_slopes, query_heads, preferred_element_type=jnp.float32
    )
    key_term = (key_term * row_scale).astype(jnp.bfloat16).reshape(row_dev, col_total, model_width)
    value_term = jnp.einsum(
        "hij,rihe->rjhe", tied_half, mixed_heads, preferred_element_type=jnp.float32
    )
    value_term = value_term.astype(jnp.bfloat16).reshape(row_dev, col_total, model_width)
    key_total, value_total = (
        lax.psum_scatter(key_term, "col", scatter_dimension=1, tiled=True).astype(jnp.float32),
        lax.psum_scatter(value_term, "col", scatter_dimension=1, tiled=True).astype(jnp.float32),
    )
    return (
        query_row_grad,
        key_total.astype(jnp.bfloat16),
        value_total.astype(jnp.bfloat16),
        query_col_back,
        key_col_back,
    )


def solution(mesh):
    placed = (
        P("seq", "col", None),
        P("seq", "col", None),
        P("seq", "col", None),
        P("seq", "col", None),
        P("seq", "col", None),
        P("seq", "col", None),
    )
    return jax.shard_map(
        on_device,
        mesh=mesh,
        in_specs=placed,
        out_specs=(
            P("seq", "col", None),
            P("seq", "col", None),
            P("seq", "col", None),
            P("seq", "col", None),
            P("seq", "col", None),
        ),
        check_vma=False,
    )
```

profile of v0, /device:TPU:1, one launch (start us, length us, event | category | flops | bytes accessed | tf_op | source)
XLA Modules:
  0.0 980.7 jit_solution(10882567209236878807)
XLA Ops:
  7.2 2.7 copy.98
  10.0 1.6 copy.112
  11.6 2.0 copy.99
  13.6 9.2 all-to-all-start
  22.9 2.0 copy.101
  24.9 20.3 %all-to-all-done = bf16[8,128,768]{2,0,1:T(8,128)(2,1)S(1)} async-done(((bf16[8,128,768]{2,0,1:T(8,128)(2,1)}), bf16[8,128,768]{2,0,1:T(8,128)(2,1)S(1)}, u32[]{:S(2)}, u32[]{:S(2)}) %all-to-all-start) | async-done | bytes 1572896 | tf_op jit(solution)/shard_map/all_to_all | solution.py:45
  45.2 4.1 all-to-all-start.1
  49.3 3.4 copy.105
  52.7 18.6 %all-to-all-done.1 = bf16[8,128,768]{2,0,1:T(8,128)(2,1)S(1)} async-done(((bf16[8,128,768]{2,0,1:T(8,128)(2,1)}), bf16[8,128,768]{2,0,1:T(8,128)(2,1)S(1)}, u32[]{:S(2)}, u32[]{:S(2)}) %all-to-all-start.1) | async-done | bytes 1572896 | tf_op jit(solution)/shard_map/all_to_all | solution.py:46
  71.3 5.2 all-to-all-start.2
  76.7 1.9 copy.97
  81.4 17.4 %all-to-all-done.2 = bf16[8,128,768]{2,0,1:T(8,128)(2,1)} async-done(((bf16[8,128,768]{2,0,1:T(8,128)(2,1)}), bf16[8,128,768]{2,0,1:T(8,128)(2,1)}, u32[]{:S(2)}, u32[]{:S(2)}) %all-to-all-start.2) | async-done | bytes 1572896 | tf_op jit(solution)/shard_map/all_to_all | solution.py:47
  98.8 2.7 copy.172
  101.4 5.9 reshape.70
  107.3 5.3 copy.108
  112.6 3.9 reshape.69
  116.5 4.4 copy.104
  120.9 6.2 reshape.68
  127.1 5.5 copy.103
  132.6 10.3 %fusion.42 = (f32[4,12,256]{2,1,0:T(8,128)S(1)}, f32[4,12,256,256]{2,3,1,0:T(8,128)}) fusion(bf16[256,4,12,64]{0,3,2,1:T(8,128)(2,1)} %copy.103, bf16[256,4,12,64]{0,3,2,1:T(8,128)(2,1)S(1)} %copy.104), kind=kOutput, calls=%fused_computation.51 | convolution fusion | flops 412090624 | bytes 15777792 | tf_op jit(solution)/shard_map/sub | solution.py:13
  142.9 5.5 convolution_bitcast_fusion
  149.9 6.6 fusion.20
  157.8 27.4 %all_to_all.111 = bf16[256,4,768]{2,1,0:T(4,128)(2,1)S(1)} all-to-all(bf16[256,4,768]{2,1,0:T(4,128)(2,1)S(1)} %copy.109), channel_id=1, replica_groups=mesh['seq'=32,'col'=4] {'seq'}, dimensions={0} | all-to-all | bytes 3145728 | tf_op jit(solution)/shard_map/all_to_all | solution.py:81
  185.5 3.9 reshape.72
  189.4 4.9 copy.113
  194.4 5.6 bitcast_convert_fusion
  200.1 268.2 %all-reduce.3.cloned.1.call-done = f32[12,128,512]{2,1,0:T(8,128)} async-done(((f32[12,128,512]{2,1,0:T(8,128)}), f32[12,128,512]{2,1,0:T(8,128)}) %all-reduce.3.cloned.1.call-update) | async-done | bytes 3145744 | tf_op jit(solution)/shard_map/psum | solution.py:38
  468.3 3.7 fusion.43
  471.9 9.1 convert_bitcast_fusion
  481.0 6.2 copy.120
  487.3 9.2 copy.149
  496.5 7.4 copy.155
  504.4 2.7 copy.117
  507.1 274.9 %all-reduce.5.cloned.1.call-done = bf16[12,128,512]{2,1,0:T(8,128)(2,1)} async-done(((bf16[12,128,512]{2,1,0:T(8,128)(2,1)}), bf16[12,128,512]{2,1,0:T(8,128)(2,1)}) %all-reduce.5.cloned.1.call-update) | async-done | bytes 1572880 | tf_op jit(solution)/shard_map/psum | solution.py:87
  781.9 2.1 fusion.12
  785.5 6.3 fusion.45
  791.8 6.5 fusion.8
  798.4 3.3 copy.118
  801.7 9.1 copy.147
  810.8 7.9 copy.153
  818.7 7.0 copy.114
  825.8 7.6 fusion.26
  835.1 22.6 %all_to_all.112 = bf16[8,128,768]{2,0,1:T(8,128)(2,1)S(1)} all-to-all(bf16[8,128,768]{2,0,1:T(8,128)(2,1)S(1)} %copy.123), channel_id=1, replica_groups=mesh['seq'=32,'col'=4] {'seq'}, dimensions={1} | all-to-all | bytes 3145728 | tf_op jit(solution)/shard_map/all_to_all | solution.py:48
  857.7 3.9 reshape.78
  861.6 7.6 fusion.2
  869.2 6.5 fusion.4
  875.7 2.0 multiply_convert_fusion.1
  878.4 2.2 copy.134
  880.6 4.0 all-to-all-start.6
  884.5 5.1 multiply_convert_fusion.2
  889.7 3.7 copy.129
  893.4 6.5 all-to-all-done.6
  899.9 4.0 all-to-all-start.5
  903.9 4.1 copy.115
  908.0 1.8 fusion.44
  911.4 2.6 copy.137
  914.4 1.4 copy.141
  915.8 6.9 all-to-all-done.5
  923.2 1.4 copy.140
  924.6 1.7 copy.156
  926.4 1.4 copy.139
  927.8 42.7 %reduce-scatter.7.cloned.1.call-done = bf16[128,6144]{1,0:T(8,128)(2,1)} async-done(((bf16[512,6144]{1,0:T(8,128)(2,1)}), bf16[128,6144]{1,0:T(8,128)(2,1)}) %reduce-scatter.7.cloned.1.call-update) | async-done | bytes 1572880
  970.5 1.7 copy.154
  972.3 1.4 copy.138
  (65 shorter events, 12.9 us)
Async XLA Ops:
  7.2 2.8 copy-start.11
  7.2 135.7 %all-gather.3.cloned.1.call-start = ((), (), s32[]{:S(2)}) async-start(), calls=%async_computation.9 | async-start | bytes 7864320 | tf_op jit(solution)/shard_map/all_gather | solution.py:28
  9.9 1.7 copy-start.12
  9.9 184.4 %all-gather.5.cloned.1.call-start = ((), (), s32[]{:S(2)}) async-start(), calls=%async_computation.11 | async-start | bytes 7864320 | tf_op jit(solution)/shard_map/all_gather | solution.py:29
  11.6 11.3 %copy-start.13 = (bf16[8,128,768]{2,1,0:T(8,128)(2,1)S(1)}, bf16[8,128,768]{2,1,0:T(8,128)(2,1)}, u32[]{:S(2)}) copy-start(bf16[8,128,768]{2,1,0:T(8,128)(2,1)} %param.10) | copy-start | bytes 4718596
  13.6 31.6 %all-to-all-start = ((bf16[8,128,768]{2,0,1:T(8,128)(2,1)}), bf16[8,128,768]{2,0,1:T(8,128)(2,1)S(1)}, u32[]{:S(2)}, u32[]{:S(2)}) async-start(bf16[8,128,768]{2,0,1:T(8,128)(2,1)} %copy.99), calls=%async_computation | async-start | bytes 3145728 | tf_op jit(solution)/shard_map/all_to_all | solution.py:45
  45.2 26.1 %all-to-all-start.1 = ((bf16[8,128,768]{2,0,1:T(8,128)(2,1)}), bf16[8,128,768]{2,0,1:T(8,128)(2,1)S(1)}, u32[]{:S(2)}, u32[]{:S(2)}) async-start(bf16[8,128,768]{2,0,1:T(8,128)(2,1)} %copy.101), calls=%async_computation.1 | async-start | bytes 3145728 | tf_op jit(solution)/shard_map/all_to_all | solution.py:46
  71.3 5.2 copy-start.7
  71.3 27.5 %all-to-all-start.2 = ((bf16[8,128,768]{2,0,1:T(8,128)(2,1)}), bf16[8,128,768]{2,0,1:T(8,128)(2,1)}, u32[]{:S(2)}, u32[]{:S(2)}) async-start(bf16[8,128,768]{2,0,1:T(8,128)(2,1)} %copy.105), calls=%async_computation.2 | async-start | bytes 3145728 | tf_op jit(solution)/shard_map/all_to_all | solution.py:47
  76.5 391.7 %all-reduce.3.cloned.1.call-start = ((), (), s32[]{:S(2)}) async-start(), calls=%async_computation.10 | async-start | bytes 6291456 | tf_op jit(solution)/shard_map/psum | solution.py:38
  78.7 64.2 %copy-start.1 = (bf16[8,128,768]{1,2,0:T(8,128)(2,1)}, bf16[8,128,768]{1,2,0:T(8,128)(2,1)S(1)}, u32[]{:S(2)}) copy-start(bf16[8,128,768]{1,2,0:T(8,128)(2,1)S(1)} %copy.97) | copy-start | bytes 4718596
  78.7 2.6 copy-start.8
  120.9 11.8 %copy-start.4 = (bf16[256,4,12,64]{0,3,2,1:T(8,128)(2,1)}, bf16[256,4,12,64]{0,3,2,1:T(8,128)(2,1)S(1)}, u32[]{:S(2)}) copy-start(bf16[256,4,12,64]{0,3,2,1:T(8,128)(2,1)S(1)} %copy.104) | copy-start | bytes 4718596
  148.4 1.5 copy-start.14
  148.5 633.5 %all-reduce.5.cloned.1.call-start = ((), (), s32[]{:S(2)}) async-start(), calls=%async_computation.12 | async-start | bytes 3145728 | tf_op jit(solution)/shard_map/psum | solution.py:87
  194.3 5.7 copy-start.16
  200.0 724.6 %reduce-scatter.9.cloned.1.call-start = ((), (), s32[]{:S(2)}) async-start(), calls=%async_computation.14 | async-start | bytes 7864320
  503.9 466.6 %reduce-scatter.7.cloned.1.call-start = ((), (), s32[]{:S(2)}) async-start(), calls=%async_computation.13 | async-start | bytes 7864320
  781.9 2.2 copy-start.9
  784.1 1.4 copy-start.10
  784.8 7.0 copy-start.2
  857.7 3.9 copy-start.15
  869.2 6.5 copy-start.6
  875.7 2.6 copy-start
  878.4 6.2 copy-start.5
  880.6 19.3 %all-to-all-start.6 = ((bf16[256,4,768]{2,1,0:T(4,128)(2,1)}), bf16[256,4,768]{2,1,0:T(4,128)(2,1)S(1)}, u32[]{:S(2)}, u32[]{:S(2)}) async-start(bf16[256,4,768]{2,1,0:T(4,128)(2,1)} %copy.134), calls=%async_computation.6 | async-start | bytes 3145728 | tf_op jit(solution)/shard_map/all_to_all | solution.py:80
  899.9 22.9 %all-to-all-start.5 = ((bf16[256,4,768]{2,1,0:T(4,128)(2,1)}), bf16[256,4,768]{2,1,0:T(4,128)(2,1)S(1)}, u32[]{:S(2)}, u32[]{:S(2)}) async-start(bf16[256,4,768]{2,1,0:T(4,128)(2,1)} %copy.129), calls=%async_computation.5 | async-start | bytes 3145728 | tf_op jit(solution)/shard_map/all_to_all | solution.py:79
  903.9 4.1 copy-start.3
Sparse Core Ops, SparseCore 0:
  10.2 104.6 all-gather.2
  117.2 49.8 all-gather.4
  169.6 298.6 all-reduce.2
  471.3 310.5 all-reduce.4
  784.4 104.2 reduce-scatter.8
  891.4 79.0 reduce-scatter.6
where the time goes:
time: 987 us; the launch traced here: 981 us
  waiting for transfers between devices  656 us (66%)
  local copies, waits for them, and re-layouts  145 us (15%)
  matrix products  67.6 us (7%)
  blocking collectives  49.9 us (5%)
  starting transfers between devices  27.3 us (3%)
  other arithmetic  20.3 us (2%)
  between operations  14.7 us (1%)
    psum x1, waiting for transfers between devices, on_device(): lax.psum(partial_slopes.astype(jnp.bfloat16), 'seq').astype(jnp.float32)  275 us
    psum x1, waiting for transfers between devices, on_device(): tied = softmax_rows(lax.psum(partial_logits, 'seq') * row_scale)  268 us
    unnamed x51, local copies, waits for them, and re-layouts  63.1 us
    unnamed x8, waiting for transfers between devices  42.8 us
    all_to_all x1, blocking collectives, on_device(): lax.all_to_all(mixed_grad, 'seq', split_axis=0, concat_axis=1, tiled=True)  27.4 us
    all_to_all x1, blocking collectives, on_device(): lax.all_to_all(row_output, 'seq', split_axis=1, concat_axis=0, tiled=True)  22.6 us
    all_to_all x1, waiting for transfers between devices, on_device(): lax.all_to_all(q_col, 'seq', split_axis=1, concat_axis=0, tiled=True)  20.3 us
  transfers between devices with their start and end apart: 11, of which 8 were waited for; matrix products, arithmetic and copies ran while one was open for 23% of the time, Pallas kernels for 0%

commit v1 on v0

v1 whole, which is shorter than its diff:
```python
import math

import jax
import jax.numpy as jnp
from jax import lax
from jax.experimental import pallas as pl
from jax.experimental.pallas import tpu as pltpu
from jax.sharding import PartitionSpec as P

MESH = pl.DeviceIdType.MESH
F32 = jnp.float32
BF16 = jnp.bfloat16
NT = (((1,), (1,)), ((), ()))
NN = (((1,), (0,)), ((), ()))
TN = (((0,), (0,)), ((), ()))
ROW_SCALE = 1.0 / math.sqrt(16384.0)
COL_SCALE = 1.0 / math.sqrt(64.0)


def dot(a, b, dims):
    return lax.dot_general(a, b, dims, preferred_element_type=F32)


def swap_halves(t):
    return jnp.concatenate([t[..., 64:128], t[..., 0:64]], axis=-1)


def low_lanes(shape):
    return lax.broadcasted_iota(jnp.int32, shape, len(shape) - 1) % 128 < 64


def pack(src, dst):
    lo = low_lanes((128, 128))

    def step(r2, _):
        for half in range(2):
            base = half * 384
            first_a, first_b = src[r2, :, base : base + 128], src[r2 + 4, :, base : base + 128]
            mid_a, mid_b = src[r2, :, base + 128 : base + 256], src[r2 + 4, :, base + 128 : base + 256]
            last_a, last_b = src[r2, :, base + 256 : base + 384], src[r2 + 4, :, base + 256 : base + 384]
            turned = swap_halves(mid_b)
            even, odd = 2 * half, 2 * half + 1
            dst[even, r2, :, 0:128] = first_a
            dst[even, r2, :, 128:256] = jnp.where(lo, mid_a, turned)
            dst[even, r2, :, 256:384] = first_b
            dst[odd, r2, :, 0:128] = last_a
            dst[odd, r2, :, 128:256] = jnp.where(lo, turned, mid_a)
            dst[odd, r2, :, 256:384] = last_b
        return 0

    lax.fori_loop(0, 4, step, 0)


def unpack_kernel(*refs):
    lo = low_lanes((128, 128))
    for src, dst in zip(refs[:5], refs[5:]):
        for half in range(2):
            base = half * 384
            even, odd = 2 * half, 2 * half + 1
            mid_even, mid_odd = src[even, 0, :, 128:256], src[odd, 0, :, 128:256]
            dst[0, 0, :, base : base + 128] = src[even, 0, :, 0:128]
            dst[1, 0, :, base : base + 128] = src[even, 0, :, 256:384]
            dst[0, 0, :, base + 128 : base + 256] = jnp.where(lo, mid_even, mid_odd)
            dst[1, 0, :, base + 128 : base + 256] = swap_halves(jnp.where(lo, mid_odd, mid_even))
            dst[0, 0, :, base + 256 : base + 384] = src[odd, 0, :, 0:128]
            dst[1, 0, :, base + 256 : base + 384] = src[odd, 0, :, 256:384]


def unpack(packed):
    outs = pl.pallas_call(
        unpack_kernel,
        name="unpack",
        grid=(4,),
        out_shape=[jax.ShapeDtypeStruct((2, 4, 128, 768), BF16)] * 5,
        in_specs=[pl.BlockSpec((4, 1, 128, 384), lambda i: (0, i, 0, 0))] * 5,
        out_specs=[pl.BlockSpec((2, 1, 128, 768), lambda i: (0, i, 0, 0))] * 5,
    )(*packed)
    return tuple(o.reshape(8, 128, 768) for o in outs)


def row_products(a, b, out):
    low = low_lanes((512, 512))
    zero = jnp.zeros((512, 512), BF16)
    for pair in range(2):
        u, v = 2 * pair, 2 * pair + 1
        left = jnp.concatenate([a[u, :, 0:128], a[u, :, 256:384], a[v, :, 0:128], a[v, :, 256:384]], axis=1)
        right = jnp.concatenate([b[u, :, 0:128], b[u, :, 256:384], b[v, :, 0:128], b[v, :, 256:384]], axis=1)
        first = dot(jnp.where(low, left, zero), right, NT)
        second = dot(jnp.where(low, zero, left), right, NT)
        left = jnp.concatenate([a[u, :, 128:256], a[v, :, 128:256]], axis=1)
        right = jnp.concatenate([b[u, :, 128:256], b[v, :, 128:256]], axis=1)
        third = dot(left, right, NT)
        if pair == 0:
            out[0], out[1], out[2] = first, second, third
        else:
            out[0] += first
            out[1] += second
            out[2] += third


def row_apply(m, b, store, dims, scale=None):
    low = low_lanes((512, 256))

    def step(pair, _):
        for r2 in (2 * pair, 2 * pair + 1):
            right = jnp.concatenate([b[r2, :, 0:128], b[r2, :, 256:384]], axis=1)
            both = jnp.where(low, dot(m[0], right, dims), dot(m[1], right, dims))
            if scale is not None:
                both = both * scale
            both = both.astype(BF16)
            store(r2, 0, both[:, 0:128])
            store(r2, 2, both[:, 128:256])
        right = jnp.concatenate([b[2 * pair, :, 128:256], b[2 * pair + 1, :, 128:256]], axis=1)
        third = dot(m[2], right, dims)
        if scale is not None:
            third = third * scale
        third = third.astype(BF16)
        store(2 * pair, 1, third[:, 0:128])
        store(2 * pair + 1, 1, third[:, 128:256])
        return 0

    lax.fori_loop(0, 2, step, 0)


def by_column(src, wide, dst):
    def widen(i, _):
        rows = pl.multiple_of(i * 16, 16)
        block = src[pl.ds(rows, 16)].reshape(256, 384).astype(F32)
        for t in range(3):
            wide[t, pl.ds(pl.multiple_of(i * 256, 256), 256), :] = block[:, 128 * t : 128 * t + 128]
        return 0

    lax.fori_loop(0, 8, widen, 0)

    def gather(c, _):
        for t in range(3):
            dst[c, :, 128 * t : 128 * t + 128] = wide[t, pl.ds(c, 128, stride=16), :].astype(BF16)
        return 0

    lax.fori_loop(0, 16, gather, 0)


def by_row(wide, dst):
    def narrow(i, _):
        rows = pl.multiple_of(i * 16, 16)
        for t in range(3):
            block = wide[t, pl.ds(pl.multiple_of(i * 256, 256), 256), :]
            dst[pl.ds(rows, 16), :, 128 * t : 128 * t + 128] = block.astype(BF16).reshape(16, 16, 128)
        return 0

    lax.fori_loop(0, 8, narrow, 0)


def stacks(ref, c):
    outer = jnp.concatenate([ref[c, :, 0:128], ref[c, :, 256:384]], axis=0)
    mid = ref[c, :, 128:256]
    return outer, jnp.concatenate([mid, swap_halves(mid)], axis=0)


def keep(x, low):
    lo = low_lanes(x.shape)
    zero = jnp.zeros_like(x)
    return jnp.where(lo, x, zero) if low else jnp.where(lo, zero, x)


def col_probs(keys, queries):
    scores = dot(keys, queries, NT) * COL_SCALE
    weights = jnp.exp(scores - jnp.max(scores, axis=0, keepdims=True))
    return weights / jnp.sum(weights, axis=0, keepdims=True)


def put_column(wide, c, p_part, q_part, w_part):
    lo = low_lanes((256, 128))
    outer = jnp.where(lo, p_part, q_part)
    rows = pl.ds(c, 128, stride=16)
    wide[0, rows, :] = outer[0:128]
    wide[2, rows, :] = outer[128:256]
    wide[1, rows, :] = jnp.where(lo[0:128], w_part[0:128], swap_halves(w_part[128:256]))


def main_kernel(
    q_row, k_row, v_row, q_col, k_col, out_grad,
    o_qr, o_kr, o_vr, o_qc, o_kc,
    stage, sends, rq, rk, rv, cq, ck, co, cro, rmix,
    part, core_l, core_g, sum_l, half_g, sum_g, tied_f, tied, slopes,
    wide0, wide1, col_q, col_k, col_o, col_r,
    load_sem, in_send, in_recv, plane_send, plane_recv, core_send, core_recv, out_send, out_recv,
):
    s, g = lax.axis_index("seq"), lax.axis_index("col")
    x, y, zl = (s // 2) % 4, s // 8, s % 2
    zh, core = g // 2, g % 2
    z = 2 * zh + zl
    chip = y * 4 + x
    slab = core * 16 + chip

    def dev(x_, y_, z_, core_):
        return (y_ * 8 + x_ * 2 + z_ % 2, (z_ // 2) * 2 + core_)

    def is_me(d):
        return jnp.logical_and(d[0] == s, d[1] == g)

    def push(src, dst, send_sem, recv_sem, dest, maybe_me=True):
        def remote():
            pltpu.make_async_remote_copy(
                src_ref=src, dst_ref=dst, send_sem=send_sem, recv_sem=recv_sem, device_id=dest, device_id_type=MESH
            ).start()

        if not maybe_me:
            remote()
            return
        me = is_me(dest)
        pl.when(jnp.logical_not(me))(remote)

        @pl.when(me)
        def _():
            pltpu.make_async_copy(src, dst, recv_sem).start()

    def wait_for(ref, sem):
        pltpu.make_async_copy(ref, ref, sem).wait()

    def loop(n, body):
        def step(i, _):
            body(i)
            return 0

        lax.fori_loop(0, n, step, 0)

    def row_dest(i):
        return dev(x, y, (z + i) % 4, zl)

    def row_home(i):
        return dev(x, y, 2 * (i // 2) + core, i % 2), i

    def col_dest(i):
        m = (i // 4 + s) % 8
        z_ = (z + i) % 4
        return dev(m % 4, 2 * core + m // 4, z_, zh), m, z_

    def col_home(i):
        j = (s + i) % 32
        return (j, core * 2 + y // 2), j

    def plane_dest(i):
        x_, y_, core_ = (x + i) % 4, (y + (i // 4)) % 4, (core + i // 16) % 2
        return dev(x_, y_, z, core_), x_, y_, core_

    barrier = pltpu.get_barrier_semaphore()

    def greet(dest):
        @pl.when(jnp.logical_not(is_me(dest)))
        def _():
            pl.semaphore_signal(barrier, inc=1, device_id=dest, device_id_type=MESH)

    arrays = (q_row, k_row, q_col, k_col, out_grad, v_row)

    def load(n):
        return pltpu.make_async_copy(arrays[n], stage.at[n % 2], load_sem.at[n % 2])

    load(0).start()
    load(1).start()
    loop(4, lambda i: greet(row_dest(i)))
    loop(4, lambda i: greet(row_home(i)[0]))
    loop(32, lambda i: greet(col_dest(i)[0]))
    loop(32, lambda i: greet(col_home(i)[0]))
    loop(32, lambda i: greet(plane_dest(i)[0]))
    own = jnp.where(core == zl, 2, 0) + jnp.where(jnp.logical_and(core == zh, y // 2 == core), 2, 0)
    pl.semaphore_wait(barrier, 103 - own)

    def send_rows(n, dst):
        def body(i):
            z_ = (z + i) % 4
            push(sends.at[n, z_], dst.at[:, pl.ds(pl.multiple_of(g * 128, 128), 128), :],
                 in_send.at[n], in_recv.at[n], row_dest(i))

        loop(4, body)

    def send_cols(n, dst):
        def body(i):
            dest, m, z_ = col_dest(i)
            push(sends.at[n, z_, :, pl.ds(pl.multiple_of(m * 16, 16), 16), :],
                 dst.at[pl.ds(4 * s, 4)], in_send.at[n], in_recv.at[n], dest)

        loop(32, body)

    for n, dst in enumerate((rq, rk, cq, ck, co, rv)):
        load(n).wait()
        pack(stage.at[n % 2], sends.at[n])
        if n + 2 < 6:
            load(n + 2).start()
        if n in (0, 1, 5):
            send_rows(n, dst)
        else:
            send_cols(n, dst)

    own_rows = pl.ds(pl.multiple_of(core * 256, 256), 256)
    other_rows = pl.ds(pl.multiple_of((1 - core) * 256, 256), 256)
    own_slab = pl.ds(pl.multiple_of(slab * 16, 16), 16)
    other_core = dev(x, y, z, 1 - core)

    def wait_plane(n, ref, other):
        wait_for(ref, plane_send.at[n])
        wait_for(other, plane_recv.at[n])

    wait_for(rq, in_recv.at[0])
    wait_for(rk, in_recv.at[1])
    row_products(rq, rk, part)
    push(part.at[:, other_rows, :], core_l, core_send.at[0], core_recv.at[0], other_core, False)
    wait_for(core_l, core_recv.at[0])
    part[:, own_rows, :] += core_l[...]

    def send_sum(i, src, dst, n):
        dest, x_, y_, _ = plane_dest(i)
        rows = pl.ds(pl.multiple_of((y_ * 4 + x_) * 16, 16), 16)
        push(src(rows, y_ * 4 + x_), dst.at[chip], plane_send.at[n], plane_recv.at[n], dest)

    def part_rows(rows, n):
        return part.at[:, pl.ds(pl.multiple_of(core * 256 + n * 16, 16), 16), :]

    loop(16, lambda i: send_sum(i, part_rows, sum_l, 0))
    wait_for(sum_l, plane_recv.at[0])
    logits = sum_l[0]
    for n in range(1, 16):
        logits += sum_l[n]
    logits = logits * ROW_SCALE
    weights = jnp.exp(logits - jnp.max(logits, axis=-1, keepdims=True))
    probs = weights / jnp.sum(weights, axis=-1, keepdims=True)
    tied_f[...] = probs

    def share(value, dst, n, core_n):
        dst[:, own_slab, :] = value.astype(BF16)
        loop(15, lambda i: push(dst.at[:, own_slab, :], dst.at[:, own_slab, :], plane_send.at[n], plane_recv.at[n],
                                plane_dest(i + 1)[0], False))
        wait_for(dst.at[:, 0:240, :], plane_recv.at[n])
        push(dst.at[:, own_rows, :], dst.at[:, own_rows, :], core_send.at[core_n], core_recv.at[core_n], other_core, False)
        wait_for(dst.at[:, 0:256, :], core_recv.at[core_n])

    share(probs, tied, 1, 1)

    wait_for(rv, in_recv.at[5])

    def wait_sent_in(n, chunk, count, mine):
        @pl.when(mine)
        def _():
            wait_for(chunk(count - 1), in_send.at[n])

        @pl.when(jnp.logical_not(mine))
        def _():
            wait_for(chunk(count), in_send.at[n])

    row_mine = core == zl
    col_mine = jnp.logical_and(core == zh, y // 2 == core)
    wait_sent_in(5, lambda k: sends.at[5, 0:k], 4, row_mine)

    ro = sends.at[5]

    def put_ro(r2, tile, value):
        for b in range(4):
            ro[r2, b, :, tile * 128 : tile * 128 + 128] = value[128 * b : 128 * b + 128]

    row_apply(tied, rv, put_ro, NN)

    def send_ro(i):
        dest, x_, y_, core_ = plane_dest(i)
        t = core_ * 16 + y_ * 4 + x_
        push(ro.at[:, t // 8, pl.ds(pl.multiple_of((t % 8) * 16, 16), 16), :], cro.at[pl.ds(4 * (chip * 2 + core), 4)],
             plane_send.at[2], plane_recv.at[2], dest)

    loop(32, send_ro)

    wait_for(cq, in_recv.at[2])
    wait_for(ck, in_recv.at[3])
    wait_for(co, in_recv.at[4])
    by_column(cq, wide0, col_q)
    by_column(ck, wide0, col_k)
    by_column(co, wide0, col_o)

    def first_pass(c):
        q, qw = stacks(col_q, c)
        k, kw = stacks(col_k, c)
        o, ow = stacks(col_o, c)
        parts = []
        for keys, queries, cot in ((k, keep(q, True), o), (k, keep(q, False), o), (kw, keep(qw, True), ow)):
            parts.append(dot(col_probs(keys, queries).astype(BF16), cot, NN))
        put_column(wide1, c, *parts)

    loop(16, first_pass)
    by_row(wide1, cq)

    def send_col(src, dst, send_sem, recv_sem):
        def body(i):
            dest, x_, y_, core_ = plane_dest(i)
            push(src.at[pl.ds(4 * ((y_ * 4 + x_) * 2 + core_), 4)], dst.at[:, own_slab, :], send_sem, recv_sem, dest)

        loop(32, body)

    send_col(cq, rmix, plane_send.at[3], plane_recv.at[3])

    wait_for(cro, plane_recv.at[2])
    by_column(cro, wide0, col_r)

    def second_pass(c):
        q, qw = stacks(col_q, c)
        k, kw = stacks(col_k, c)
        o, ow = stacks(col_o, c)
        r, rw = stacks(col_r, c)
        q_parts, k_parts = [], []
        for keys, queries, cot, vals, low in ((k, q, o, r, True), (k, q, o, r, False), (kw, qw, ow, rw, True)):
            probs = col_probs(keys, keep(queries, low))
            grads = dot(vals, keep(cot, low), NT)
            slope = probs * (grads - jnp.sum(probs * grads, axis=0, keepdims=True))
            slope = slope.astype(BF16)
            k_parts.append(dot(slope, queries, NN) * COL_SCALE)
            q_parts.append(dot(slope, keys, TN) * COL_SCALE)
        put_column(wide0, c, *q_parts)
        put_column(wide1, c, *k_parts)

    loop(16, second_pass)
    by_row(wide0, ck)
    by_row(wide1, co)

    def send_home(src, dst, n):
        def body(i):
            dest, j = col_home(i)
            push(src.at[pl.ds(4 * j, 4)], dst.at[z, :, pl.ds(pl.multiple_of((slab % 8) * 16, 16), 16), :],
                 out_send.at[n], out_recv.at[n], dest)

        loop(32, body)

    send_home(ck, o_qc, 3)
    send_home(co, o_kc, 4)

    wait_for(rmix, plane_recv.at[3])
    wait_for(part.at[:, 0:256, :], core_send.at[0])
    wait_for(sum_l.at[0:15], plane_send.at[0])
    row_products(rmix, rv, part)
    push(part.at[:, other_rows, :], core_g, core_send.at[2], core_recv.at[2], other_core, False)
    wait_for(core_g, core_recv.at[2])
    half_g[...] = (part[:, own_rows, :] + core_g[...]).astype(BF16)

    def half_rows(rows, n):
        return half_g.at[:, rows, :]

    loop(16, lambda i: send_sum(i, half_rows, sum_g, 4))

    def in_place(ref):
        def store(r2, tile, value):
            ref[r2, :, tile * 128 : tile * 128 + 128] = value

        return store

    def send_rows_home(src, dst, n):
        def body(i):
            dest, b = row_home(i)
            push(src.at[:, pl.ds(pl.multiple_of(b * 128, 128), 128), :], dst.at[z], out_send.at[n], out_recv.at[n], dest)

        loop(4, body)

    row_apply(tied, rmix, in_place(rmix), TN)
    send_rows_home(rmix, o_vr, 2)

    wait_for(sum_g, plane_recv.at[4])
    grads = sum_g[0].astype(F32)
    for n in range(1, 16):
        grads += sum_g[n].astype(F32)
    probs = tied_f[...]
    slope = probs * (grads - jnp.sum(probs * grads, axis=-1, keepdims=True))
    share(slope, slopes, 5, 3)

    row_apply(slopes, rk, in_place(rk), NN, ROW_SCALE)
    send_rows_home(rk, o_qr, 0)
    row_apply(slopes, rq, in_place(rq), TN, ROW_SCALE)
    send_rows_home(rq, o_kr, 1)

    for n in (0, 1):
        wait_sent_in(n, lambda k, n=n: sends.at[n, 0:k], 4, row_mine)
    for n in (2, 3, 4):
        wait_sent_in(n, lambda k: cq.at[0 : 4 * k], 32, col_mine)
    wait_for(tied.at[:, 0:240, :], plane_send.at[1])
    wait_for(cro.at[0:124], plane_send.at[2])
    wait_for(cro.at[0:124], plane_send.at[3])
    wait_for(sum_g.at[0:15], plane_send.at[4])
    wait_for(tied.at[:, 0:240, :], plane_send.at[5])
    wait_for(tied.at[:, 0:256, :], core_send.at[1])
    wait_for(core_g, core_send.at[2])
    wait_for(tied.at[:, 0:256, :], core_send.at[3])

    def wait_out(n, chunk, count, mine):
        @pl.when(mine)
        def _():
            wait_for(chunk(count - 1), out_send.at[n])

        @pl.when(jnp.logical_not(mine))
        def _():
            wait_for(chunk(count), out_send.at[n])

    for n, ref in enumerate((o_qr, o_kr, o_vr, o_qc, o_kc)):
        if n < 3:
            wait_out(n, lambda k: sends.at[n, 0:k], 4, row_mine)
        else:
            wait_out(n, lambda k: cq.at[0 : 4 * k], 32, col_mine)
        wait_for(ref, out_recv.at[n])


def on_device(q_row, k_row, v_row, q_col, k_col, out_grad):
    vm = pltpu.VMEM
    dma = pltpu.SemaphoreType.DMA
    rows, cols = (4, 512, 384), (128, 16, 384)
    packed = pl.pallas_call(
        main_kernel,
        name="layer",
        out_shape=[jax.ShapeDtypeStruct((4, 4, 128, 384), BF16)] * 5,
        in_specs=[pl.BlockSpec(memory_space=pl.ANY)] * 6,
        out_specs=[pl.BlockSpec(memory_space=pl.ANY)] * 5,
        scratch_shapes=[
            vm((2, 8, 128, 768), BF16),
            vm((6, 4, 4, 128, 384), BF16),
            vm(rows, BF16), vm(rows, BF16), vm(rows, BF16),
            vm(cols, BF16), vm(cols, BF16), vm(cols, BF16), vm(cols, BF16),
            vm(rows, BF16),
            vm((3, 512, 512), F32),
            vm((3, 256, 512), F32), vm((3, 256, 512), F32),
            vm((16, 3, 16, 512), F32),
            vm((3, 256, 512), BF16),
            vm((16, 3, 16, 512), BF16),
            vm((3, 16, 512), F32),
            vm((3, 512, 512), BF16), vm((3, 512, 512), BF16),
            vm((3, 2048, 128), F32), vm((3, 2048, 128), F32),
            vm((16, 128, 384), BF16), vm((16, 128, 384), BF16), vm((16, 128, 384), BF16), vm((16, 128, 384), BF16),
            dma((2,)), dma((6,)), dma((6,)), dma((6,)), dma((6,)), dma((4,)), dma((4,)), dma((5,)), dma((5,)),
        ],
        compiler_params=pltpu.CompilerParams(collective_id=0, has_side_effects=True, vmem_limit_bytes=62 << 20),
    )(q_row, k_row, v_row, q_col, k_col, out_grad)
    return unpack(packed)


def solution(mesh):
    spec = P("seq", "col", None)
    return jax.shard_map(on_device, mesh=mesh, in_specs=(spec,) * 6, out_specs=(spec,) * 5, check_vma=False)
```

time: 987 us -> 304 us (0.31)
  waiting for transfers between devices: 656 us -> 0 us
  Pallas kernels: 0 us -> 303 us
  local copies, waits for them, and re-layouts: 145 us -> 0 us
  matrix products: 67.6 us -> 0 us
  blocking collectives: 49.9 us -> 0 us
  starting transfers between devices: 27.3 us -> 0 us
  other arithmetic: 20.3 us -> 0 us
  between operations: 14.7 us -> 0.64 us
    psum x2 -> x0, waiting for transfers between devices: 543 us -> none  [the longest x1 275 us: on_device(): lax.psum(partial_slopes.astype(jnp.bfloat16), 'seq').astype(jnp.float32)]
    pallas_call x0 -> x2, Pallas kernels: none -> 303 us  [the longest x1 296 us: on_device(): pl.pallas_call(main_kernel, name='layer', out_shape=[jax.ShapeDtypeStruct...]
    all_to_all x5 -> x0, waiting for transfers between devices: 69.7 us -> none  [the longest x1 20.3 us: on_device(): lax.all_to_all(q_col, 'seq', split_axis=1, concat_axis=0, tiled=True)]
    reshape x16 -> x0, local copies, waits for them, and re-layouts: 65.9 us -> none  [the longest x2 11.8 us: on_device(): col_query = col_query.reshape(head_shape)]
    unnamed x51 -> x0, local copies, waits for them, and re-layouts: 63.1 us -> none
    all_to_all x2 -> x0, blocking collectives: 49.9 us -> none  [the longest x1 27.4 us: on_device(): lax.all_to_all(mixed_grad, 'seq', split_axis=0, concat_axis=1, tiled=True)]
    unnamed x8 -> x0, waiting for transfers between devices: 42.8 us -> none
    dot_general x7 -> x0, matrix products: 41.6 us -> none  [the longest x1 9.08 us: on_device(): jnp.einsum('hij,rihe->rjhe', tied_half, mixed_heads, preferred_element_ty...]
  transfers between devices with their start and end apart: 11 -> 0, of which waited for: 8 -> 0; matrix products, arithmetic and copies ran while one was open for 23% -> 0% of each run, Pallas kernels for 0% -> 0%
where the time goes in v1:
time: 304 us
  Pallas kernels  303 us (100%)
    pallas_call x1, Pallas kernels, on_device(): pl.pallas_call(main_kernel, name='layer', out_shape=[jax.ShapeDtypeStruct...  296 us
    pallas_call x1, Pallas kernels, unpack(): pl.pallas_call(unpack_kernel, name='unpack', grid=(4,), out_shape=[jax.Sh...  7.17 us

profile of v1, /device:TPU:1, one launch (start us, length us, event | category | flops | bytes accessed | tf_op | source)
XLA Modules:
  0.0 303.6 jit_solution(4787658033661150541)
XLA Ops:
  0.6 295.8 %layer.1 = (bf16[4,4,128,384]{3,2,1,0:T(8,128)(2,1)}, bf16[4,4,128,384]{3,2,1,0:T(8,128)(2,1)}, bf16[4,4,128,384]{3,2,1,0:T(8,128)(2,1)}, bf16[4,4,128,384]{3,2,1,0:T(8,128)(2,1)}, bf16[4,4,128,384]{3,2,1,0:T(8,128)(2,1)}) custom-call(bf16[8,128,768]{2,1,0:T(8,128)(2,1)} %q_row.1, bf16[8,128,768]{2,1,0:T(8,128)(2,1)} %k_row.1, bf16[8,128,768]{2,1,0:T(8,128)(2,1)} %v_row.1, ...), custom_call_target="tpu_custom_call" | custom-call | tf_op jit(solution)/shard_map/layer/pallas_call | solution.py:508
  296.4 7.2 %unpack.1 = (bf16[2,4,128,768]{3,2,1,0:T(8,128)(2,1)}, bf16[2,4,128,768]{3,2,1,0:T(8,128)(2,1)}, bf16[2,4,128,768]{3,2,1,0:T(8,128)(2,1)}, bf16[2,4,128,768]{3,2,1,0:T(8,128)(2,1)}, bf16[2,4,128,768]{3,2,1,0:T(8,128)(2,1)}) custom-call(bf16[4,4,128,384]{3,2,1,0:T(8,128)(2,1)} %get-tuple-element.15.refs_0_, ...), custom_call_target="tpu_custom_call" | custom-call | tf_op jit(solution)/shard_map/unpack/pallas_call | solution.py:70

commit v2 on v1

v2 whole, which is shorter than its diff:
```python
import math

import jax
import jax.numpy as jnp
from jax import lax
from jax.experimental import pallas as pl
from jax.experimental.pallas import tpu as pltpu
from jax.sharding import PartitionSpec as P

MESH = pl.DeviceIdType.MESH
F32 = jnp.float32
BF16 = jnp.bfloat16
NT = (((1,), (1,)), ((), ()))
NN = (((1,), (0,)), ((), ()))
TN = (((0,), (0,)), ((), ()))
ROW_SCALE = 1.0 / math.sqrt(16384.0)
COL_SCALE = 1.0 / math.sqrt(64.0)


def dot(a, b, dims):
    return lax.dot_general(a, b, dims, preferred_element_type=F32)


def swap_halves(t):
    return jnp.concatenate([t[..., 64:128], t[..., 0:64]], axis=-1)


def low_lanes(shape):
    return lax.broadcasted_iota(jnp.int32, shape, len(shape) - 1) % 128 < 64


def pack(src, dst):
    lo = low_lanes((128, 128))

    def step(r2, _):
        for half in range(2):
            base = half * 384
            mid_a, mid_b = src[r2, :, base + 128 : base + 256], src[r2 + 4, :, base + 128 : base + 256]
            turned = swap_halves(mid_b)
            even, odd = 2 * half, 2 * half + 1
            dst[even, r2, :, 0:128] = src[r2, :, base : base + 128]
            dst[even, r2, :, 128:256] = src[r2 + 4, :, base : base + 128]
            dst[even, r2, :, 256:384] = jnp.where(lo, mid_a, turned)
            dst[odd, r2, :, 0:128] = src[r2, :, base + 256 : base + 384]
            dst[odd, r2, :, 128:256] = src[r2 + 4, :, base + 256 : base + 384]
            dst[odd, r2, :, 256:384] = jnp.where(lo, turned, mid_a)
        return 0

    lax.fori_loop(0, 4, step, 0)


def unpack_kernel(*refs):
    lo = low_lanes((128, 128))
    for src, dst in zip(refs[:5], refs[5:]):
        for half in range(2):
            base = half * 384
            even, odd = 2 * half, 2 * half + 1
            mid_even, mid_odd = src[even, 0, :, 256:384], src[odd, 0, :, 256:384]
            dst[0, 0, :, base : base + 128] = src[even, 0, :, 0:128]
            dst[1, 0, :, base : base + 128] = src[even, 0, :, 128:256]
            dst[0, 0, :, base + 128 : base + 256] = jnp.where(lo, mid_even, mid_odd)
            dst[1, 0, :, base + 128 : base + 256] = swap_halves(jnp.where(lo, mid_odd, mid_even))
            dst[0, 0, :, base + 256 : base + 384] = src[odd, 0, :, 0:128]
            dst[1, 0, :, base + 256 : base + 384] = src[odd, 0, :, 128:256]


def unpack(packed):
    outs = pl.pallas_call(
        unpack_kernel,
        name="unpack",
        grid=(4,),
        out_shape=[jax.ShapeDtypeStruct((2, 4, 128, 768), BF16)] * 5,
        in_specs=[pl.BlockSpec((4, 1, 128, 384), lambda i: (0, i, 0, 0))] * 5,
        out_specs=[pl.BlockSpec((2, 1, 128, 768), lambda i: (0, i, 0, 0))] * 5,
    )(*packed)
    return tuple(o.reshape(8, 128, 768) for o in outs)


def row_products(a, b, out):
    low = low_lanes((512, 512))
    zero = jnp.zeros((512, 512), BF16)
    for pair in range(2):
        u, v = 2 * pair, 2 * pair + 1
        left = jnp.concatenate([a[u, :, 0:256], a[v, :, 0:256]], axis=1)
        right = jnp.concatenate([b[u, :, 0:256], b[v, :, 0:256]], axis=1)
        first = dot(jnp.where(low, left, zero), right, NT)
        second = dot(jnp.where(low, zero, left), right, NT)
        left = jnp.concatenate([a[u, :, 256:384], a[v, :, 256:384]], axis=1)
        right = jnp.concatenate([b[u, :, 256:384], b[v, :, 256:384]], axis=1)
        third = dot(left, right, NT)
        if pair == 0:
            out[0], out[1], out[2] = first, second, third
        else:
            out[0] += first
            out[1] += second
            out[2] += third


def row_apply(m, b, store, dims, scale=None):
    low = low_lanes((512, 256))

    def step(pair, _):
        for r2 in (2 * pair, 2 * pair + 1):
            right = b[r2, :, 0:256]
            both = jnp.where(low, dot(m[0], right, dims), dot(m[1], right, dims))
            if scale is not None:
                both = both * scale
            both = both.astype(BF16)
            store(r2, 0, both[:, 0:128])
            store(r2, 1, both[:, 128:256])
        right = jnp.concatenate([b[2 * pair, :, 256:384], b[2 * pair + 1, :, 256:384]], axis=1)
        third = dot(m[2], right, dims)
        if scale is not None:
            third = third * scale
        third = third.astype(BF16)
        store(2 * pair, 2, third[:, 0:128])
        store(2 * pair + 1, 2, third[:, 128:256])
        return 0

    lax.fori_loop(0, 2, step, 0)


def by_column(src, wide, dst):
    def widen(i, _):
        block = src[i // 4, pl.ds((i % 4) * 4, 4)].reshape(256, 384).astype(F32)
        for t in range(3):
            wide[t, pl.ds(pl.multiple_of(i * 256, 256), 256), :] = block[:, 128 * t : 128 * t + 128]
        return 0

    lax.fori_loop(0, 8, widen, 0)

    def gather(c, _):
        for t in range(3):
            dst[c, :, 128 * t : 128 * t + 128] = wide[t, pl.ds(c, 128, stride=16), :].astype(BF16)
        return 0

    lax.fori_loop(0, 16, gather, 0)


def by_row(wide, dst, tiles):
    def narrow(i, _):
        for t in tiles:
            block = wide[t, pl.ds(pl.multiple_of(i * 256, 256), 256), :].astype(BF16)
            dst[i // 4, pl.ds((i % 4) * 4, 4), :, :, 128 * t : 128 * t + 128] = block.reshape(4, 4, 16, 128)
        return 0

    lax.fori_loop(0, 8, narrow, 0)


def outer_rows(ref, c):
    return jnp.concatenate([ref[c, :, 0:128], ref[c, :, 128:256]], axis=0)


def mid_rows(ref, c):
    mid = ref[c, :, 256:384]
    return jnp.concatenate([mid, swap_halves(mid)], axis=0)


def keep(x, low):
    lo = low_lanes(x.shape)
    zero = jnp.zeros_like(x)
    return jnp.where(lo, x, zero) if low else jnp.where(lo, zero, x)


HEADS = ((outer_rows, True), (outer_rows, False), (mid_rows, True))


def put_outer(wide, c, p_part, q_part):
    outer = jnp.where(low_lanes((256, 128)), p_part, q_part)
    rows = pl.ds(c, 128, stride=16)
    wide[0, rows, :] = outer[0:128]
    wide[1, rows, :] = outer[128:256]


def put_mid(wide, c, part):
    wide[2, pl.ds(c, 128, stride=16), :] = jnp.where(low_lanes((128, 128)), part[0:128], swap_halves(part[128:256]))


def main_kernel(
    q_row, k_row, v_row, q_col, k_col, out_grad,
    o_qr, o_kr, o_vr, o_qc, o_kc,
    stage, sends, rq, rk, rv, mq, mk, mo, cq, ck, co, cro, rmix,
    part, core_l, core_g, sum_l, half_g, sum_g, tied_f, tied, slopes,
    wide0, wide1, col_q, col_k, col_o, col_r, norms,
    load_sem, in_send, in_recv, on_send, on_recv, plane_send, plane_recv, core_send, core_recv, out_send, out_recv,
):
    s, g = lax.axis_index("seq"), lax.axis_index("col")
    x, y, zl = (s // 2) % 4, s // 8, s % 2
    zh, core = g // 2, g % 2
    z = 2 * zh + zl
    chip = y * 4 + x
    slab = core * 16 + chip

    def dev(x_, y_, z_, core_):
        return (y_ * 8 + x_ * 2 + z_ % 2, (z_ // 2) * 2 + core_)

    def is_me(d):
        return jnp.logical_and(d[0] == s, d[1] == g)

    def push(src, dst, send_sem, recv_sem, dest, maybe_me=True):
        def remote():
            pltpu.make_async_remote_copy(
                src_ref=src, dst_ref=dst, send_sem=send_sem, recv_sem=recv_sem, device_id=dest, device_id_type=MESH
            ).start()

        if not maybe_me:
            remote()
            return
        me = is_me(dest)
        pl.when(jnp.logical_not(me))(remote)

        @pl.when(me)
        def _():
            pltpu.make_async_copy(src, dst, recv_sem).start()

    def wait_for(ref, sem):
        pltpu.make_async_copy(ref, ref, sem).wait()

    def wait_sent(sem, chunks, count, mine):
        @pl.when(mine)
        def _():
            wait_for(chunks(count - 1), sem)

        @pl.when(jnp.logical_not(mine))
        def _():
            wait_for(chunks(count), sem)

    def loop(n, body):
        def step(i, _):
            body(i)
            return 0

        lax.fori_loop(0, n, step, 0)

    row_mine = core == zl
    plane_mine = y // 2 == core
    line_mine = core == zh
    home_mine = jnp.logical_and(line_mine, plane_mine)

    def row_dest(i):
        return dev(x, y, (z + i) % 4, zl)

    def row_home(i):
        return dev(x, y, 2 * (i // 2) + core, i % 2), i

    def col_dest(i):
        m = (i // 4 + s) % 8
        return dev(m % 4, 2 * core + m // 4, (z + i) % 4, zh)

    def col_home(i):
        j = (s + i) % 32
        return (j, core * 2 + y // 2), j

    def plane_dest(i):
        x_, y_, core_ = (x + i) % 4, (y + (i // 4)) % 4, (core + i // 16) % 2
        return dev(x_, y_, z, core_), x_, y_, core_

    barrier = pltpu.get_barrier_semaphore()

    def greet(dest):
        @pl.when(jnp.logical_not(is_me(dest)))
        def _():
            pl.semaphore_signal(barrier, inc=1, device_id=dest, device_id_type=MESH)

    arrays = (q_row, k_row, q_col, k_col, out_grad, v_row)

    def load(n):
        return pltpu.make_async_copy(arrays[n], stage.at[n % 2], load_sem.at[n % 2])

    def pack_next(n):
        load(n).wait()
        pack(stage.at[n % 2], sends.at[n])
        if n + 2 < 6:
            load(n + 2).start()

    load(0).start()
    load(1).start()
    loop(6, lambda i: greet(dev(x, y, (z + 1 + i // 2) % 4, i % 2)))
    loop(31, lambda i: greet(plane_dest(i + 1)[0]))
    loop(32, lambda i: greet(col_dest(i)))
    loop(32, lambda i: greet(col_home(i)[0]))
    pack_next(0)
    pack_next(1)
    pack_next(2)
    pl.semaphore_wait(barrier, 101 - jnp.where(home_mine, 2, 0))

    def send_rows(n, dst):
        def body(i):
            z_ = (z + i) % 4
            push(sends.at[n, z_], dst.at[:, pl.ds(pl.multiple_of(g * 128, 128), 128), :],
                 in_send.at[n], in_recv.at[n], row_dest(i))

        loop(4, body)

    def send_plane(n, dst):
        def body(i):
            x_, half, core_ = (x + i) % 4, (y + i // 4) % 2, (core + i // 8) % 2
            push(sends.at[n, pl.ds(2 * core_, 2), :, pl.ds(pl.multiple_of((half * 4 + x_) * 16, 16), 16), :],
                 dst.at[:, chip], in_send.at[n], in_recv.at[n], dev(x_, 2 * core + half, z, core_))

        loop(16, body)

    def send_line(n, src, dst):
        def body(i):
            j = (i + zl) % 2
            push(src.at[j], dst.at[zl], on_send.at[n], on_recv.at[n], dev(x, y, 2 * core + j, zh))

        loop(2, body)

    def wait_in(n):
        if n in (0, 1, 5):
            wait_sent(in_send.at[n], lambda k: sends.at[n, 0:k], 4, row_mine)
        else:
            wait_sent(in_send.at[n], lambda k: mq.at[:, 0:k], 16, plane_mine)

    own_rows = pl.ds(pl.multiple_of(core * 256, 256), 256)
    other_rows = pl.ds(pl.multiple_of((1 - core) * 256, 256), 256)
    own_slab = pl.ds(pl.multiple_of(slab * 16, 16), 16)
    other_core = dev(x, y, z, 1 - core)

    def send_sum(src, dst, n):
        def body(i):
            dest, x_, y_, _ = plane_dest(i)
            push(src(y_ * 4 + x_), dst.at[chip], plane_send.at[n], plane_recv.at[n], dest)

        loop(16, body)

    def share(value, dst, n):
        dst[:, own_slab, :] = value.astype(BF16)
        loop(15, lambda i: push(dst.at[:, own_slab, :], dst.at[:, own_slab, :], plane_send.at[n], plane_recv.at[n],
                                plane_dest(i + 1)[0], False))

    def share_core(dst, n, core_n):
        wait_for(dst.at[:, 0:240, :], plane_recv.at[n])
        push(dst.at[:, own_rows, :], dst.at[:, own_rows, :], core_send.at[core_n], core_recv.at[core_n], other_core, False)
        wait_for(dst.at[:, 0:256, :], core_recv.at[core_n])

    send_rows(0, rq)
    send_rows(1, rk)
    send_plane(2, mq)
    pack_next(3)
    send_plane(3, mk)
    pack_next(4)
    pack_next(5)
    wait_in(0)
    send_rows(5, rv)
    wait_in(2)
    send_plane(4, mo)

    wait_for(rq, in_recv.at[0])
    wait_for(rk, in_recv.at[1])
    row_products(rq, rk, part)
    push(part.at[:, other_rows, :], core_l, core_send.at[0], core_recv.at[0], other_core, False)
    wait_for(mq, in_recv.at[2])
    send_line(0, mq, cq)
    wait_for(core_l, core_recv.at[0])
    part[:, own_rows, :] += core_l[...]
    send_sum(lambda n: part.at[:, pl.ds(pl.multiple_of(core * 256 + n * 16, 16), 16), :], sum_l, 0)
    wait_for(mk, in_recv.at[3])
    send_line(1, mk, ck)
    wait_for(sum_l, plane_recv.at[0])
    logits = sum_l[0]
    for n in range(1, 16):
        logits += sum_l[n]
    logits = logits * ROW_SCALE
    weights = jnp.exp(logits - jnp.max(logits, axis=-1, keepdims=True))
    probs = weights / jnp.sum(weights, axis=-1, keepdims=True)
    tied_f[...] = probs
    share(probs, tied, 1)
    wait_for(mo, in_recv.at[4])
    send_line(2, mo, co)
    share_core(tied, 1, 1)

    wait_for(rv, in_recv.at[5])
    wait_in(5)
    ro = sends.at[5]

    def put_ro(r2, tile, value):
        for b in range(4):
            ro[r2, b, :, tile * 128 : tile * 128 + 128] = value[128 * b : 128 * b + 128]

    row_apply(tied, rv, put_ro, NN)

    def send_ro(i):
        dest, x_, y_, core_ = plane_dest(i)
        t = core_ * 16 + y_ * 4 + x_
        push(ro.at[:, t // 8, pl.ds(pl.multiple_of((t % 8) * 16, 16), 16), :], cro.at[core, chip],
             plane_send.at[2], plane_recv.at[2], dest)

    loop(32, send_ro)

    for n in (1, 3, 4):
        wait_in(n)
    wait_for(cq, on_recv.at[0])
    by_column(cq, wide0, col_q)
    wait_for(ck, on_recv.at[1])
    by_column(ck, wide0, col_k)

    def put_probs(c, h, value):
        for half in range(2):
            rows = value[128 * half : 128 * half + 128]
            if h == 0:
                sends[c // 4, c % 4, half, :, 0:256] = rows
            elif h == 1:
                sends[c // 4, c % 4, half, :, 256:384] = rows[:, 0:128]
                sends[c // 4, c % 4, 2 + half, :, 0:128] = rows[:, 128:256]
            else:
                sends[c // 4, c % 4, 2 + half, :, 128:384] = rows

    def get_probs(c, h):
        rows = []
        for half in range(2):
            if h == 0:
                rows.append(sends[c // 4, c % 4, half, :, 0:256])
            elif h == 1:
                rows.append(jnp.concatenate([sends[c // 4, c % 4, half, :, 256:384], sends[c // 4, c % 4, 2 + half, :, 0:128]], axis=1))
            else:
                rows.append(sends[c // 4, c % 4, 2 + half, :, 128:384])
        return jnp.concatenate(rows, axis=0)

    def probs_pass(c):
        logs = []
        for h, (rows, low) in enumerate(HEADS):
            scores = dot(rows(col_k, c), keep(rows(col_q, c), low), NT) * COL_SCALE
            top = jnp.max(scores, axis=0, keepdims=True)
            weights = jnp.exp(scores - top)
            total = jnp.sum(weights, axis=0, keepdims=True)
            put_probs(c, h, (weights * (1.0 / total)).astype(BF16))
            logs.append(top + jnp.log(total))
        norms[c] = jnp.concatenate(logs, axis=0)

    loop(16, probs_pass)

    wait_for(co, on_recv.at[2])
    by_column(co, wide0, col_o)

    def mixed_pass(c):
        outer = outer_rows(col_o, c)
        put_outer(wide1, c, dot(get_probs(c, 0), outer, NN), dot(get_probs(c, 1), outer, NN))
        put_mid(wide1, c, dot(get_probs(c, 2), mid_rows(col_o, c), NN))

    loop(16, mixed_pass)
    by_row(wide1, cq, (0, 1, 2))

    def send_mixed(i):
        dest, x_, y_, core_ = plane_dest(i)
        push(cq.at[core_, y_ * 4 + x_], rmix.at[:, own_slab, :], plane_send.at[3], plane_recv.at[3], dest)

    loop(32, send_mixed)

    wait_for(cro, plane_recv.at[2])
    by_column(cro, wide0, col_r)

    def slope_parts(c, h):
        rows, low = HEADS[h]
        queries, keys = rows(col_q, c), rows(col_k, c)
        scores = dot(keys, keep(queries, low), NT) * COL_SCALE
        probs = jnp.exp(scores - norms[c, h : h + 1, :])
        grads = dot(rows(col_r, c), keep(rows(col_o, c), low), NT)
        slope = probs * (grads - jnp.sum(probs * grads, axis=0, keepdims=True))
        slope = slope.astype(BF16)
        return dot(slope, keys, TN) * COL_SCALE, dot(slope, queries, NN) * COL_SCALE

    def mid_pass(c):
        q_part, k_part = slope_parts(c, 2)
        put_mid(wide0, c, q_part)
        put_mid(wide1, c, k_part)

    def outer_pass(c):
        q_p, k_p = slope_parts(c, 0)
        q_q, k_q = slope_parts(c, 1)
        put_outer(wide0, c, q_p, q_q)
        put_outer(wide1, c, k_p, k_q)

    def send_home(src, dst, n, lanes):
        def body(i):
            dest, j = col_home(i)
            push(src.at[j % 2, j // 2, :, :, lanes],
                 dst.at[z, :, pl.ds(pl.multiple_of((slab % 8) * 16, 16), 16), lanes],
                 out_send.at[n], out_recv.at[n], dest)

        loop(32, body)

    mid, outer = pl.ds(256, 128), pl.ds(0, 256)
    loop(16, mid_pass)
    by_row(wide0, ck, (2,))
    by_row(wide1, co, (2,))
    send_home(ck, o_qc, 5, mid)
    send_home(co, o_kc, 6, mid)
    loop(16, outer_pass)
    by_row(wide0, ck, (0, 1))
    by_row(wide1, co, (0, 1))
    send_home(ck, o_qc, 3, outer)
    send_home(co, o_kc, 4, outer)

    wait_for(rmix, plane_recv.at[3])
    wait_for(part.at[:, 0:256, :], core_send.at[0])
    wait_for(sum_l.at[0:15], plane_send.at[0])
    row_products(rmix, rv, part)
    push(part.at[:, other_rows, :], core_g, core_send.at[2], core_recv.at[2], other_core, False)

    def in_place(ref):
        def store(r2, tile, value):
            ref[r2, :, tile * 128 : tile * 128 + 128] = value

        return store

    def send_rows_home(src, dst, n):
        def body(i):
            dest, b = row_home(i)
            push(src.at[:, pl.ds(pl.multiple_of(b * 128, 128), 128), :], dst.at[z], out_send.at[n], out_recv.at[n], dest)

        loop(4, body)

    row_apply(tied, rmix, in_place(rmix), TN)
    wait_for(core_g, core_recv.at[2])
    half_g[...] = (part[:, own_rows, :] + core_g[...]).astype(BF16)
    send_sum(lambda n: half_g.at[:, pl.ds(pl.multiple_of(n * 16, 16), 16), :], sum_g, 4)
    send_rows_home(rmix, o_vr, 2)
    wait_for(sum_g, plane_recv.at[4])
    grads = sum_g[0].astype(F32)
    for n in range(1, 16):
        grads += sum_g[n].astype(F32)
    probs = tied_f[...]
    share(probs * (grads - jnp.sum(probs * grads, axis=-1, keepdims=True)), slopes, 5)
    share_core(slopes, 5, 3)

    row_apply(slopes, rk, in_place(rk), NN, ROW_SCALE)
    send_rows_home(rk, o_qr, 0)
    row_apply(slopes, rq, in_place(rq), TN, ROW_SCALE)
    send_rows_home(rq, o_kr, 1)

    for n in range(3):
        wait_sent(on_send.at[n], lambda k: mq.at[0:k], 2, line_mine)
    wait_for(tied.at[:, 0:240, :], plane_send.at[1])
    wait_for(rq.at[:, 0:496, :], plane_send.at[2])
    wait_for(rq.at[:, 0:496, :], plane_send.at[3])
    wait_for(sum_g.at[0:15], plane_send.at[4])
    wait_for(tied.at[:, 0:240, :], plane_send.at[5])
    wait_for(tied.at[:, 0:256, :], core_send.at[1])
    wait_for(core_g, core_send.at[2])
    wait_for(tied.at[:, 0:256, :], core_send.at[3])
    for n, ref in enumerate((o_qr, o_kr, o_vr)):
        wait_sent(out_send.at[n], lambda k: sends.at[0, 0:k], 4, row_mine)
        wait_for(ref, out_recv.at[n])
    for n, ref, lanes in ((5, o_qc, mid), (6, o_kc, mid), (3, o_qc, outer), (4, o_kc, outer)):
        wait_sent(out_send.at[n], lambda k: rq.at[:, 0 : 16 * k, lanes], 32, home_mine)
        wait_for(ref.at[:, :, :, lanes], out_recv.at[n])


def on_device(q_row, k_row, v_row, q_col, k_col, out_grad):
    vm = pltpu.VMEM
    dma = pltpu.SemaphoreType.DMA
    rows, cols = (4, 512, 384), (2, 16, 4, 16, 384)
    packed = pl.pallas_call(
        main_kernel,
        name="layer",
        out_shape=[jax.ShapeDtypeStruct((4, 4, 128, 384), BF16)] * 5,
        in_specs=[pl.BlockSpec(memory_space=pl.ANY)] * 6,
        out_specs=[pl.BlockSpec(memory_space=pl.ANY)] * 5,
        scratch_shapes=[
            vm((2, 8, 128, 768), BF16),
            vm((6, 4, 4, 128, 384), BF16),
            vm(rows, BF16), vm(rows, BF16), vm(rows, BF16),
            vm(cols, BF16), vm(cols, BF16), vm(cols, BF16),
            vm(cols, BF16), vm(cols, BF16), vm(cols, BF16), vm(cols, BF16),
            vm(rows, BF16),
            vm((3, 512, 512), F32),
            vm((3, 256, 512), F32), vm((3, 256, 512), F32),
            vm((16, 3, 16, 512), F32),
            vm((3, 256, 512), BF16),
            vm((16, 3, 16, 512), BF16),
            vm((3, 16, 512), F32),
            vm((3, 512, 512), BF16), vm((3, 512, 512), BF16),
            vm((3, 2048, 128), F32), vm((3, 2048, 128), F32),
            vm((16, 128, 384), BF16), vm((16, 128, 384), BF16), vm((16, 128, 384), BF16), vm((16, 128, 384), BF16),
            vm((16, 3, 256), F32),
            dma((2,)), dma((6,)), dma((6,)), dma((3,)), dma((3,)), dma((6,)), dma((6,)), dma((4,)), dma((4,)),
            dma((7,)), dma((7,)),
        ],
        compiler_params=pltpu.CompilerParams(collective_id=0, has_side_effects=True, vmem_limit_bytes=62 << 20),
    )(q_row, k_row, v_row, q_col, k_col, out_grad)
    return unpack(packed)


def solution(mesh):
    spec = P("seq", "col", None)
    return jax.shard_map(on_device, mesh=mesh, in_specs=(spec,) * 6, out_specs=(spec,) * 5, check_vma=False)
```

time: 304 us -> 255 us (0.84)
  Pallas kernels: 303 us -> 254 us
    pallas_call x1, Pallas kernels: 296 us -> 247 us  [on_device(): pl.pallas_call(main_kernel, name='layer', out_shape=[jax.ShapeDtypeStruct...]
where the time goes in v2:
time: 255 us
  Pallas kernels  254 us (100%)
    pallas_call x1, Pallas kernels, on_device(): pl.pallas_call(main_kernel, name='layer', out_shape=[jax.ShapeDtypeStruct...  247 us
    pallas_call x1, Pallas kernels, unpack(): pl.pallas_call(unpack_kernel, name='unpack', grid=(4,), out_shape=[jax.Sh...  7.17 us

profile of v2, /device:TPU:1, one launch (start us, length us, event | category | flops | bytes accessed | tf_op | source)
XLA Modules:
  0.0 255.1 jit_solution(11565377076370537284)
XLA Ops:
  0.6 247.2 %layer.1 = (bf16[4,4,128,384]{3,2,1,0:T(8,128)(2,1)}, bf16[4,4,128,384]{3,2,1,0:T(8,128)(2,1)}, bf16[4,4,128,384]{3,2,1,0:T(8,128)(2,1)}, bf16[4,4,128,384]{3,2,1,0:T(8,128)(2,1)}, bf16[4,4,128,384]{3,2,1,0:T(8,128)(2,1)}) custom-call(bf16[8,128,768]{2,1,0:T(8,128)(2,1)} %q_row.1, bf16[8,128,768]{2,1,0:T(8,128)(2,1)} %k_row.1, bf16[8,128,768]{2,1,0:T(8,128)(2,1)} %v_row.1, ...), custom_call_target="tpu_custom_call" | custom-call | tf_op jit(solution)/shard_map/layer/pallas_call | solution.py:555
  247.9 7.2 %unpack.1 = (bf16[2,4,128,768]{3,2,1,0:T(8,128)(2,1)}, bf16[2,4,128,768]{3,2,1,0:T(8,128)(2,1)}, bf16[2,4,128,768]{3,2,1,0:T(8,128)(2,1)}, bf16[2,4,128,768]{3,2,1,0:T(8,128)(2,1)}, bf16[2,4,128,768]{3,2,1,0:T(8,128)(2,1)}) custom-call(bf16[4,4,128,384]{3,2,1,0:T(8,128)(2,1)} %get-tuple-element.15.refs_0_, ...), custom_call_target="tpu_custom_call" | custom-call | tf_op jit(solution)/shard_map/unpack/pallas_call | solution.py:68

commit v3 on v2

--- a/solution.py
+++ b/solution.py
@@ -52,48 +52,47 @@
 def unpack_kernel(*refs):
     lo = low_lanes((128, 128))
     for src, dst in zip(refs[:5], refs[5:]):
-        for half in range(2):
+        for half, k in ((0, 0), (0, 1), (1, 0), (1, 1)):
             base = half * 384
             even, odd = 2 * half, 2 * half + 1
-            mid_even, mid_odd = src[even, 0, :, 256:384], src[odd, 0, :, 256:384]
-            dst[0, 0, :, base : base + 128] = src[even, 0, :, 0:128]
-            dst[1, 0, :, base : base + 128] = src[even, 0, :, 128:256]
-            dst[0, 0, :, base + 128 : base + 256] = jnp.where(lo, mid_even, mid_odd)
-            dst[1, 0, :, base + 128 : base + 256] = swap_halves(jnp.where(lo, mid_odd, mid_even))
-            dst[0, 0, :, base + 256 : base + 384] = src[odd, 0, :, 0:128]
-            dst[1, 0, :, base + 256 : base + 384] = src[odd, 0, :, 128:256]
+            mid_even, mid_odd = src[even, k, :, 256:384], src[odd, k, :, 256:384]
+            dst[0, k, :, base : base + 128] = src[even, k, :, 0:128]
+            dst[1, k, :, base : base + 128] = src[even, k, :, 128:256]
+            dst[0, k, :, base + 128 : base + 256] = jnp.where(lo, mid_even, mid_odd)
+            dst[1, k, :, base + 128 : base + 256] = swap_halves(jnp.where(lo, mid_odd, mid_even))
+            dst[0, k, :, base + 256 : base + 384] = src[odd, k, :, 0:128]
+            dst[1, k, :, base + 256 : base + 384] = src[odd, k, :, 128:256]
 
 
 def unpack(packed):
     outs = pl.pallas_call(
         unpack_kernel,
         name="unpack",
-        grid=(4,),
+        grid=(2,),
         out_shape=[jax.ShapeDtypeStruct((2, 4, 128, 768), BF16)] * 5,
-        in_specs=[pl.BlockSpec((4, 1, 128, 384), lambda i: (0, i, 0, 0))] * 5,
-        out_specs=[pl.BlockSpec((2, 1, 128, 768), lambda i: (0, i, 0, 0))] * 5,
+        in_specs=[pl.BlockSpec((4, 2, 128, 384), lambda i: (0, i, 0, 0))] * 5,
+        out_specs=[pl.BlockSpec((2, 2, 128, 768), lambda i: (0, i, 0, 0))] * 5,
+        compiler_params=pltpu.CompilerParams(vmem_limit_bytes=62 << 20),
     )(*packed)
     return tuple(o.reshape(8, 128, 768) for o in outs)
 
 
-def row_products(a, b, out):
+def row_product(a, b, out, h):
     low = low_lanes((512, 512))
     zero = jnp.zeros((512, 512), BF16)
-    for pair in range(2):
-        u, v = 2 * pair, 2 * pair + 1
-        left = jnp.concatenate([a[u, :, 0:256], a[v, :, 0:256]], axis=1)
-        right = jnp.concatenate([b[u, :, 0:256], b[v, :, 0:256]], axis=1)
-        first = dot(jnp.where(low, left, zero), right, NT)
-        second = dot(jnp.where(low, zero, left), right, NT)
-        left = jnp.concatenate([a[u, :, 256:384], a[v, :, 256:384]], axis=1)
-        right = jnp.concatenate([b[u, :, 256:384], b[v, :, 256:384]], axis=1)
-        third = dot(left, right, NT)
-        if pair == 0:
-            out[0], out[1], out[2] = first, second, third
-        else:
-            out[0] += first
-            out[1] += second
-            out[2] += third
+    total = None
+    if h < 2:
+        for u in (0, 2):
+            left = jnp.concatenate([a[u, :, 0:256], a[u + 1, :, 0:256]], axis=1)
+            right = jnp.concatenate([b[u, :, 0:256], b[u + 1, :, 0:256]], axis=1)
+            left = jnp.where(low, left, zero) if h == 0 else jnp.where(low, zero, left)
+            term = dot(left, right, NT)
+            total = term if total is None else total + term
+    else:
+        left = jnp.concatenate([a[u, :, 256:384] for u in range(4)], axis=1)
+        right = jnp.concatenate([b[u, :, 256:384] for u in range(4)], axis=1)
+        total = dot(left, right, NT)
+    out[h] = total
 
 
 def row_apply(m, b, store, dims, scale=None):
@@ -130,8 +129,12 @@
     lax.fori_loop(0, 8, widen, 0)
 
     def gather(c, _):
-        for t in range(3):
-            dst[c, :, 128 * t : 128 * t + 128] = wide[t, pl.ds(c, 128, stride=16), :].astype(BF16)
+        rows = pl.ds(c, 128, stride=16)
+        mid = wide[2, rows, :]
+        dst[c, 0:128, 0:128] = wide[0, rows, :].astype(BF16)
+        dst[c, 128:256, 0:128] = wide[1, rows, :].astype(BF16)
+        dst[c, 0:128, 128:256] = mid.astype(BF16)
+        dst[c, 128:256, 128:256] = pltpu.roll(mid, 64, 1).astype(BF16)
         return 0
 
     lax.fori_loop(0, 16, gather, 0)
@@ -148,12 +151,11 @@
 
 
 def outer_rows(ref, c):
-    return jnp.concatenate([ref[c, :, 0:128], ref[c, :, 128:256]], axis=0)
+    return ref[c, :, 0:128]
 
 
 def mid_rows(ref, c):
-    mid = ref[c, :, 256:384]
-    return jnp.concatenate([mid, swap_halves(mid)], axis=0)
+    return ref[c, :, 128:256]
 
 
 def keep(x, low):
@@ -173,7 +175,7 @@
 
 
 def put_mid(wide, c, part):
-    wide[2, pl.ds(c, 128, stride=16), :] = jnp.where(low_lanes((128, 128)), part[0:128], swap_halves(part[128:256]))
+    wide[2, pl.ds(c, 128, stride=16), :] = jnp.where(low_lanes((128, 128)), part[0:128], pltpu.roll(part[128:256], 64, 1))
 
 
 def main_kernel(
@@ -232,6 +234,13 @@
 
         lax.fori_loop(0, n, step, 0)
 
+    def columns(body):
+        def four(i):
+            for j in range(4):
+                body(4 * i + j)
+
+        loop(4, four)
+
     row_mine = core == zl
     plane_mine = y // 2 == core
     line_mine = core == zh
@@ -326,14 +335,28 @@
         loop(16, body)
 
     def share(value, dst, n):
-        dst[:, own_slab, :] = value.astype(BF16)
-        loop(15, lambda i: push(dst.at[:, own_slab, :], dst.at[:, own_slab, :], plane_send.at[n], plane_recv.at[n],
+        dst[own_slab, :] = value.astype(BF16)
+        loop(15, lambda i: push(dst.at[own_slab, :], dst.at[own_slab, :], plane_send.at[n], plane_recv.at[n],
                                 plane_dest(i + 1)[0], False))
 
     def share_core(dst, n, core_n):
-        wait_for(dst.at[:, 0:240, :], plane_recv.at[n])
-        push(dst.at[:, own_rows, :], dst.at[:, own_rows, :], core_send.at[core_n], core_recv.at[core_n], other_core, False)
-        wait_for(dst.at[:, 0:256, :], core_recv.at[core_n])
+        for h in range(3):
+            wait_for(dst.at[h, 0:240, :], plane_recv.at[n + h])
+            push(dst.at[h, own_rows, :], dst.at[h, own_rows, :], core_send.at[core_n + h], core_recv.at[core_n + h],
+                 other_core, False)
+        for h in range(3):
+            wait_for(dst.at[h, 0:256, :], core_recv.at[core_n + h])
+
+    def products(a, b, inbox, core_n):
+        for h in range(3):
+            row_product(a, b, part, h)
+            push(part.at[h, other_rows, :], inbox.at[h], core_send.at[core_n + h], core_recv.at[core_n + h], other_core, False)
+
+    def add_up(ref):
+        total = ref[0].astype(F32)
+        for n in range(1, 16):
+            total += ref[n].astype(F32)
+        return total
 
     send_rows(0, rq)
     send_rows(1, rk)
@@ -349,27 +372,25 @@
 
     wait_for(rq, in_recv.at[0])
     wait_for(rk, in_recv.at[1])
-    row_products(rq, rk, part)
-    push(part.at[:, other_rows, :], core_l, core_send.at[0], core_recv.at[0], other_core, False)
+    products(rq, rk, core_l, 0)
     wait_for(mq, in_recv.at[2])
     send_line(0, mq, cq)
-    wait_for(core_l, core_recv.at[0])
-    part[:, own_rows, :] += core_l[...]
-    send_sum(lambda n: part.at[:, pl.ds(pl.multiple_of(core * 256 + n * 16, 16), 16), :], sum_l, 0)
+    for h in range(3):
+        wait_for(core_l.at[h], core_recv.at[h])
+        part[h, own_rows, :] += core_l[h]
+        send_sum(lambda n: part.at[h, pl.ds(pl.multiple_of(core * 256 + n * 16, 16), 16), :], sum_l.at[h], h)
     wait_for(mk, in_recv.at[3])
     send_line(1, mk, ck)
-    wait_for(sum_l, plane_recv.at[0])
-    logits = sum_l[0]
-    for n in range(1, 16):
-        logits += sum_l[n]
-    logits = logits * ROW_SCALE
-    weights = jnp.exp(logits - jnp.max(logits, axis=-1, keepdims=True))
-    probs = weights / jnp.sum(weights, axis=-1, keepdims=True)
-    tied_f[...] = probs
-    share(probs, tied, 1)
+    for h in range(3):
+        wait_for(sum_l.at[h], plane_recv.at[h])
+        logits = add_up(sum_l.at[h]) * ROW_SCALE
+        weights = jnp.exp(logits - jnp.max(logits, axis=-1, keepdims=True))
+        probs = weights / jnp.sum(weights, axis=-1, keepdims=True)
+        tied_f[h] = probs
+        share(probs, tied.at[h], 3 + h)
     wait_for(mo, in_recv.at[4])
     send_line(2, mo, co)
-    share_core(tied, 1, 1)
+    share_core(tied, 3, 3)
 
     wait_for(rv, in_recv.at[5])
     wait_in(5)
@@ -385,7 +406,7 @@
         dest, x_, y_, core_ = plane_dest(i)
         t = core_ * 16 + y_ * 4 + x_
         push(ro.at[:, t // 8, pl.ds(pl.multiple_of((t % 8) * 16, 16), 16), :], cro.at[core, chip],
-             plane_send.at[2], plane_recv.at[2], dest)
+             plane_send.at[6], plane_recv.at[6], dest)
 
     loop(32, send_ro)
 
@@ -429,7 +450,7 @@
             logs.append(top + jnp.log(total))
         norms[c] = jnp.concatenate(logs, axis=0)
 
-    loop(16, probs_pass)
+    columns(probs_pass)
 
     wait_for(co, on_recv.at[2])
     by_column(co, wide0, col_o)
@@ -439,16 +460,16 @@
         put_outer(wide1, c, dot(get_probs(c, 0), outer, NN), dot(get_probs(c, 1), outer, NN))
         put_mid(wide1, c, dot(get_probs(c, 2), mid_rows(col_o, c), NN))
 
-    loop(16, mixed_pass)
+    columns(mixed_pass)
     by_row(wide1, cq, (0, 1, 2))
 
     def send_mixed(i):
         dest, x_, y_, core_ = plane_dest(i)
-        push(cq.at[core_, y_ * 4 + x_], rmix.at[:, own_slab, :], plane_send.at[3], plane_recv.at[3], dest)
+        push(cq.at[core_, y_ * 4 + x_], rmix.at[:, own_slab, :], plane_send.at[7], plane_recv.at[7], dest)
 
     loop(32, send_mixed)
 
-    wait_for(cro, plane_recv.at[2])
+    wait_for(cro, plane_recv.at[6])
     by_column(cro, wide0, col_r)
 
     def slope_parts(c, h):
@@ -482,22 +503,22 @@
         loop(32, body)
 
     mid, outer = pl.ds(256, 128), pl.ds(0, 256)
-    loop(16, mid_pass)
+    columns(mid_pass)
     by_row(wide0, ck, (2,))
     by_row(wide1, co, (2,))
     send_home(ck, o_qc, 5, mid)
     send_home(co, o_kc, 6, mid)
-    loop(16, outer_pass)
+    columns(outer_pass)
     by_row(wide0, ck, (0, 1))
     by_row(wide1, co, (0, 1))
     send_home(ck, o_qc, 3, outer)
     send_home(co, o_kc, 4, outer)
 
-    wait_for(rmix, plane_recv.at[3])
-    wait_for(part.at[:, 0:256, :], core_send.at[0])
-    wait_for(sum_l.at[0:15], plane_send.at[0])
-    row_products(rmix, rv, part)
-    push(part.at[:, other_rows, :], core_g, core_send.at[2], core_recv.at[2], other_core, False)
+    wait_for(rmix, plane_recv.at[7])
+    for h in range(3):
+        wait_for(part.at[h, 0:256, :], core_send.at[h])
+        wait_for(sum_l.at[h, 0:15], plane_send.at[h])
+    products(rmix, rv, core_g, 6)
 
     def in_place(ref):
         def store(r2, tile, value):
@@ -512,18 +533,18 @@
 
         loop(4, body)
 
+    for h in range(3):
+        wait_for(core_g.at[h], core_recv.at[6 + h])
+        half_g[h] = (part[h, own_rows, :] + core_g[h]).astype(BF16)
+        send_sum(lambda n: half_g.at[h, pl.ds(pl.multiple_of(n * 16, 16), 16), :], sum_g.at[h], 8 + h)
     row_apply(tied, rmix, in_place(rmix), TN)
-    wait_for(core_g, core_recv.at[2])
-    half_g[...] = (part[:, own_rows, :] + core_g[...]).astype(BF16)
-    send_sum(lambda n: half_g.at[:, pl.ds(pl.multiple_of(n * 16, 16), 16), :], sum_g, 4)
     send_rows_home(rmix, o_vr, 2)
-    wait_for(sum_g, plane_recv.at[4])
-    grads = sum_g[0].astype(F32)
-    for n in range(1, 16):
-        grads += sum_g[n].astype(F32)
-    probs = tied_f[...]
-    share(probs * (grads - jnp.sum(probs * grads, axis=-1, keepdims=True)), slopes, 5)
-    share_core(slopes, 5, 3)
+    for h in range(3):
+        wait_for(sum_g.at[h], plane_recv.at[8 + h])
+        grads = add_up(sum_g.at[h])
+        probs = tied_f[h]
+        share(probs * (grads - jnp.sum(probs * grads, axis=-1, keepdims=True)), slopes.at[h], 11 + h)
+    share_core(slopes, 11, 9)
 
     row_apply(slopes, rk, in_place(rk), NN, ROW_SCALE)
     send_rows_home(rk, o_qr, 0)
@@ -532,14 +553,15 @@
 
     for n in range(3):
         wait_sent(on_send.at[n], lambda k: mq.at[0:k], 2, line_mine)
-    wait_for(tied.at[:, 0:240, :], plane_send.at[1])
-    wait_for(rq.at[:, 0:496, :], plane_send.at[2])
-    wait_for(rq.at[:, 0:496, :], plane_send.at[3])
-    wait_for(sum_g.at[0:15], plane_send.at[4])
-    wait_for(tied.at[:, 0:240, :], plane_send.at[5])
-    wait_for(tied.at[:, 0:256, :], core_send.at[1])
-    wait_for(core_g, core_send.at[2])
-    wait_for(tied.at[:, 0:256, :], core_send.at[3])
+    wait_for(rq.at[:, 0:496, :], plane_send.at[6])
+    wait_for(rq.at[:, 0:496, :], plane_send.at[7])
+    for h in range(3):
+        wait_for(tied.at[h, 0:240, :], plane_send.at[3 + h])
+        wait_for(sum_g.at[h, 0:15], plane_send.at[8 + h])
+        wait_for(tied.at[h, 0:240, :], plane_send.at[11 + h])
+        wait_for(tied.at[h, 0:256, :], core_send.at[3 + h])
+        wait_for(core_g.at[h], core_send.at[6 + h])
+        wait_for(tied.at[h, 0:256, :], core_send.at[9 + h])
     for n, ref in enumerate((o_qr, o_kr, o_vr)):
         wait_sent(out_send.at[n], lambda k: sends.at[0, 0:k], 4, row_mine)
         wait_for(ref, out_recv.at[n])
@@ -567,15 +589,15 @@
             vm(rows, BF16),
             vm((3, 512, 512), F32),
             vm((3, 256, 512), F32), vm((3, 256, 512), F32),
-            vm((16, 3, 16, 512), F32),
+            vm((3, 16, 16, 512), F32),
             vm((3, 256, 512), BF16),
-            vm((16, 3, 16, 512), BF16),
+            vm((3, 16, 16, 512), BF16),
             vm((3, 16, 512), F32),
             vm((3, 512, 512), BF16), vm((3, 512, 512), BF16),
             vm((3, 2048, 128), F32), vm((3, 2048, 128), F32),
-            vm((16, 128, 384), BF16), vm((16, 128, 384), BF16), vm((16, 128, 384), BF16), vm((16, 128, 384), BF16),
+            vm((16, 256, 256), BF16), vm((16, 256, 256), BF16), vm((16, 256, 256), BF16), vm((16, 256, 256), BF16),
             vm((16, 3, 256), F32),
-            dma((2,)), dma((6,)), dma((6,)), dma((3,)), dma((3,)), dma((6,)), dma((6,)), dma((4,)), dma((4,)),
+            dma((2,)), dma((6,)), dma((6,)), dma((3,)), dma((3,)), dma((14,)), dma((14,)), dma((12,)), dma((12,)),
             dma((7,)), dma((7,)),
         ],
         compiler_params=pltpu.CompilerParams(collective_id=0, has_side_effects=True, vmem_limit_bytes=62 << 20),

time: 255 us -> 242 us (0.949)
  Pallas kernels: 254 us -> 241 us
    pallas_call x1, Pallas kernels: 247 us -> 235 us  [on_device(): pl.pallas_call(main_kernel, name='layer', out_shape=[jax.ShapeDtypeStruct...]
where the time goes in v3:
time: 242 us
  Pallas kernels  241 us (100%)
    pallas_call x1, Pallas kernels, on_device(): pl.pallas_call(main_kernel, name='layer', out_shape=[jax.ShapeDtypeStruct...  235 us
    pallas_call x1, Pallas kernels, unpack(): pl.pallas_call(unpack_kernel, name='unpack', grid=(2,), out_shape=[jax.Sh...  6 us

profile of v3, /device:TPU:1, one launch (start us, length us, event | category | flops | bytes accessed | tf_op | source)
XLA Modules:
  0.0 242.0 jit_solution(13018936142142025743)
XLA Ops:
  0.6 235.4 %layer.1 = (bf16[4,4,128,384]{3,2,1,0:T(8,128)(2,1)}, bf16[4,4,128,384]{3,2,1,0:T(8,128)(2,1)}, bf16[4,4,128,384]{3,2,1,0:T(8,128)(2,1)}, bf16[4,4,128,384]{3,2,1,0:T(8,128)(2,1)}, bf16[4,4,128,384]{3,2,1,0:T(8,128)(2,1)}) custom-call(bf16[8,128,768]{2,1,0:T(8,128)(2,1)} %q_row.1, bf16[8,128,768]{2,1,0:T(8,128)(2,1)} %k_row.1, bf16[8,128,768]{2,1,0:T(8,128)(2,1)} %v_row.1, ...), custom_call_target="tpu_custom_call" | custom-call | tf_op jit(solution)/shard_map/layer/pallas_call | solution.py:577
  236.0 6.0 %unpack.1 = (bf16[2,4,128,768]{3,2,1,0:T(8,128)(2,1)}, bf16[2,4,128,768]{3,2,1,0:T(8,128)(2,1)}, bf16[2,4,128,768]{3,2,1,0:T(8,128)(2,1)}, bf16[2,4,128,768]{3,2,1,0:T(8,128)(2,1)}, bf16[2,4,128,768]{3,2,1,0:T(8,128)(2,1)}) custom-call(bf16[4,4,128,384]{3,2,1,0:T(8,128)(2,1)} %get-tuple-element.15.refs_0_, ...), custom_call_target="tpu_custom_call" | custom-call | tf_op jit(solution)/shard_map/unpack/pallas_call | solution.py:68

commit v4 on v3

--- a/solution.py
+++ b/solution.py
@@ -95,23 +95,28 @@
     out[h] = total
 
 
-def row_apply(m, b, store, dims, scale=None):
+def finish(value, scale):
+    return (value if scale is None else value * scale).astype(BF16)
+
+
+def apply_outer(m, b, store, dims, scale=None):
     low = low_lanes((512, 256))
 
     def step(pair, _):
         for r2 in (2 * pair, 2 * pair + 1):
             right = b[r2, :, 0:256]
-            both = jnp.where(low, dot(m[0], right, dims), dot(m[1], right, dims))
-            if scale is not None:
-                both = both * scale
-            both = both.astype(BF16)
+            both = finish(jnp.where(low, dot(m[0], right, dims), dot(m[1], right, dims)), scale)
             store(r2, 0, both[:, 0:128])
             store(r2, 1, both[:, 128:256])
+        return 0
+
+    lax.fori_loop(0, 2, step, 0)
+
+
+def apply_mid(m, b, store, dims, scale=None):
+    def step(pair, _):
         right = jnp.concatenate([b[2 * pair, :, 256:384], b[2 * pair + 1, :, 256:384]], axis=1)
-        third = dot(m[2], right, dims)
-        if scale is not None:
-            third = third * scale
-        third = third.astype(BF16)
+        third = finish(dot(m[2], right, dims), scale)
         store(2 * pair, 2, third[:, 0:128])
         store(2 * pair + 1, 2, third[:, 128:256])
         return 0
@@ -119,25 +124,33 @@
     lax.fori_loop(0, 2, step, 0)
 
 
-def by_column(src, wide, dst):
+def row_apply(*args):
+    apply_outer(*args)
+    apply_mid(*args)
+
+
+def by_column(src, wide, dst, tiles=(0, 1, 2)):
     def widen(i, _):
-        block = src[i // 4, pl.ds((i % 4) * 4, 4)].reshape(256, 384).astype(F32)
-        for t in range(3):
-            wide[t, pl.ds(pl.multiple_of(i * 256, 256), 256), :] = block[:, 128 * t : 128 * t + 128]
+        for t in tiles:
+            block = src[i // 4, pl.ds((i % 4) * 4, 4), :, :, 128 * t : 128 * t + 128]
+            wide[t, pl.ds(pl.multiple_of(i * 256, 256), 256), :] = block.reshape(256, 128).astype(F32)
         return 0
 
     lax.fori_loop(0, 8, widen, 0)
 
-    def gather(c, _):
-        rows = pl.ds(c, 128, stride=16)
-        mid = wide[2, rows, :]
-        dst[c, 0:128, 0:128] = wide[0, rows, :].astype(BF16)
-        dst[c, 128:256, 0:128] = wide[1, rows, :].astype(BF16)
-        dst[c, 0:128, 128:256] = mid.astype(BF16)
-        dst[c, 128:256, 128:256] = pltpu.roll(mid, 64, 1).astype(BF16)
+    def gather(i, _):
+        for c in (2 * i, 2 * i + 1):
+            rows = pl.ds(c, 128, stride=16)
+            for t in tiles:
+                if t < 2:
+                    dst[c, 128 * t : 128 * t + 128, 0:128] = wide[t, rows, :].astype(BF16)
+                else:
+                    mid = wide[2, rows, :]
+                    dst[c, 0:128, 128:256] = mid.astype(BF16)
+                    dst[c, 128:256, 128:256] = pltpu.roll(mid, 64, 1).astype(BF16)
         return 0
 
-    lax.fori_loop(0, 16, gather, 0)
+    lax.fori_loop(0, 8, gather, 0)
 
 
 def by_row(wide, dst, tiles):
@@ -241,6 +254,10 @@
 
         loop(4, four)
 
+    def fan(n, body):
+        body(0, True)
+        loop(n - 1, lambda i: body(i + 1, False))
+
     row_mine = core == zl
     plane_mine = y // 2 == core
     line_mine = core == zh
@@ -294,27 +311,27 @@
     pl.semaphore_wait(barrier, 101 - jnp.where(home_mine, 2, 0))
 
     def send_rows(n, dst):
-        def body(i):
+        def body(i, maybe_me):
             z_ = (z + i) % 4
             push(sends.at[n, z_], dst.at[:, pl.ds(pl.multiple_of(g * 128, 128), 128), :],
-                 in_send.at[n], in_recv.at[n], row_dest(i))
-
-        loop(4, body)
+                 in_send.at[n], in_recv.at[n], row_dest(i), maybe_me)
+
+        fan(4, body)
 
     def send_plane(n, dst):
-        def body(i):
+        def body(i, maybe_me):
             x_, half, core_ = (x + i) % 4, (y + i // 4) % 2, (core + i // 8) % 2
             push(sends.at[n, pl.ds(2 * core_, 2), :, pl.ds(pl.multiple_of((half * 4 + x_) * 16, 16), 16), :],
-                 dst.at[:, chip], in_send.at[n], in_recv.at[n], dev(x_, 2 * core + half, z, core_))
-
-        loop(16, body)
+                 dst.at[:, chip], in_send.at[n], in_recv.at[n], dev(x_, 2 * core + half, z, core_), maybe_me)
+
+        fan(16, body)
 
     def send_line(n, src, dst):
-        def body(i):
+        def body(i, maybe_me):
             j = (i + zl) % 2
-            push(src.at[j], dst.at[zl], on_send.at[n], on_recv.at[n], dev(x, y, 2 * core + j, zh))
-
-        loop(2, body)
+            push(src.at[j], dst.at[zl], on_send.at[n], on_recv.at[n], dev(x, y, 2 * core + j, zh), maybe_me)
+
+        fan(2, body)
 
     def wait_in(n):
         if n in (0, 1, 5):
@@ -328,11 +345,11 @@
     other_core = dev(x, y, z, 1 - core)
 
     def send_sum(src, dst, n):
-        def body(i):
+        def body(i, maybe_me):
             dest, x_, y_, _ = plane_dest(i)
-            push(src(y_ * 4 + x_), dst.at[chip], plane_send.at[n], plane_recv.at[n], dest)
-
-        loop(16, body)
+            push(src(y_ * 4 + x_), dst.at[chip], plane_send.at[n], plane_recv.at[n], dest, maybe_me)
+
+        fan(16, body)
 
     def share(value, dst, n):
         dst[own_slab, :] = value.astype(BF16)
@@ -400,15 +417,21 @@
         for b in range(4):
             ro[r2, b, :, tile * 128 : tile * 128 + 128] = value[128 * b : 128 * b + 128]
 
-    row_apply(tied, rv, put_ro, NN)
-
-    def send_ro(i):
-        dest, x_, y_, core_ = plane_dest(i)
-        t = core_ * 16 + y_ * 4 + x_
-        push(ro.at[:, t // 8, pl.ds(pl.multiple_of((t % 8) * 16, 16), 16), :], cro.at[core, chip],
-             plane_send.at[6], plane_recv.at[6], dest)
-
-    loop(32, send_ro)
+    mid, outer = pl.ds(256, 128), pl.ds(0, 256)
+
+    def send_ro(lanes, n):
+        def body(i, maybe_me):
+            dest, x_, y_, core_ = plane_dest(i)
+            t = core_ * 16 + y_ * 4 + x_
+            push(ro.at[:, t // 8, pl.ds(pl.multiple_of((t % 8) * 16, 16), 16), lanes], cro.at[core, chip, :, :, lanes],
+                 plane_send.at[n], plane_recv.at[n], dest, maybe_me)
+
+        fan(32, body)
+
+    apply_mid(tied, rv, put_ro, NN)
+    send_ro(mid, 14)
+    apply_outer(tied, rv, put_ro, NN)
+    send_ro(outer, 6)
 
     for n in (1, 3, 4):
         wait_in(n)
@@ -463,14 +486,14 @@
     columns(mixed_pass)
     by_row(wide1, cq, (0, 1, 2))
 
-    def send_mixed(i):
+    def send_mixed(i, maybe_me):
         dest, x_, y_, core_ = plane_dest(i)
-        push(cq.at[core_, y_ * 4 + x_], rmix.at[:, own_slab, :], plane_send.at[7], plane_recv.at[7], dest)
-
-    loop(32, send_mixed)
-
-    wait_for(cro, plane_recv.at[6])
-    by_column(cro, wide0, col_r)
+        push(cq.at[core_, y_ * 4 + x_], rmix.at[:, own_slab, :], plane_send.at[7], plane_recv.at[7], dest, maybe_me)
+
+    fan(32, send_mixed)
+
+    wait_for(cro.at[:, :, :, :, mid], plane_recv.at[14])
+    by_column(cro, wide0, col_r, (2,))
 
     def slope_parts(c, h):
         rows, low = HEADS[h]
@@ -494,25 +517,25 @@
         put_outer(wide1, c, k_p, k_q)
 
     def send_home(src, dst, n, lanes):
-        def body(i):
+        def body(i, maybe_me):
             dest, j = col_home(i)
             push(src.at[j % 2, j // 2, :, :, lanes],
                  dst.at[z, :, pl.ds(pl.multiple_of((slab % 8) * 16, 16), 16), lanes],
-                 out_send.at[n], out_recv.at[n], dest)
-
-        loop(32, body)
-
-    mid, outer = pl.ds(256, 128), pl.ds(0, 256)
+                 out_send.at[n], out_recv.at[n], dest, maybe_me)
+
+        fan(32, body)
+
     columns(mid_pass)
     by_row(wide0, ck, (2,))
+    send_home(ck, o_qc, 5, mid)
     by_row(wide1, co, (2,))
-    send_home(ck, o_qc, 5, mid)
     send_home(co, o_kc, 6, mid)
+    wait_for(cro.at[:, :, :, :, outer], plane_recv.at[6])
+    by_column(cro, wide0, col_r, (0, 1))
     columns(outer_pass)
     by_row(wide0, ck, (0, 1))
+    send_home(ck, o_qc, 3, outer)
     by_row(wide1, co, (0, 1))
-    send_home(ck, o_qc, 3, outer)
-    send_home(co, o_kc, 4, outer)
 
     wait_for(rmix, plane_recv.at[7])
     for h in range(3):
@@ -544,6 +567,7 @@
         grads = add_up(sum_g.at[h])
         probs = tied_f[h]
         share(probs * (grads - jnp.sum(probs * grads, axis=-1, keepdims=True)), slopes.at[h], 11 + h)
+    send_home(co, o_kc, 4, outer)
     share_core(slopes, 11, 9)
 
     row_apply(slopes, rk, in_place(rk), NN, ROW_SCALE)
@@ -553,7 +577,8 @@
 
     for n in range(3):
         wait_sent(on_send.at[n], lambda k: mq.at[0:k], 2, line_mine)
-    wait_for(rq.at[:, 0:496, :], plane_send.at[6])
+    wait_for(rq.at[:, 0:496, outer], plane_send.at[6])
+    wait_for(rq.at[:, 0:496, mid], plane_send.at[14])
     wait_for(rq.at[:, 0:496, :], plane_send.at[7])
     for h in range(3):
         wait_for(tied.at[h, 0:240, :], plane_send.at[3 + h])
@@ -597,7 +622,7 @@
             vm((3, 2048, 128), F32), vm((3, 2048, 128), F32),
             vm((16, 256, 256), BF16), vm((16, 256, 256), BF16), vm((16, 256, 256), BF16), vm((16, 256, 256), BF16),
             vm((16, 3, 256), F32),
-            dma((2,)), dma((6,)), dma((6,)), dma((3,)), dma((3,)), dma((14,)), dma((14,)), dma((12,)), dma((12,)),
+            dma((2,)), dma((6,)), dma((6,)), dma((3,)), dma((3,)), dma((15,)), dma((15,)), dma((12,)), dma((12,)),
             dma((7,)), dma((7,)),
         ],
         compiler_params=pltpu.CompilerParams(collective_id=0, has_side_effects=True, vmem_limit_bytes=62 << 20),

time: 242 us -> 236 us (0.975)
  Pallas kernels: 241 us -> 235 us
    pallas_call x1, Pallas kernels: 235 us -> 229 us  [on_device(): pl.pallas_call(main_kernel, name='layer', out_shape=[jax.ShapeDtypeStruct...]
where the time goes in v4:
time: 236 us
  Pallas kernels  235 us (100%)
    pallas_call x1, Pallas kernels, on_device(): pl.pallas_call(main_kernel, name='layer', out_shape=[jax.ShapeDtypeStruct...  229 us
    pallas_call x1, Pallas kernels, unpack(): pl.pallas_call(unpack_kernel, name='unpack', grid=(2,), out_shape=[jax.Sh...  6 us

profile of v4, /device:TPU:1, one launch (start us, length us, event | category | flops | bytes accessed | tf_op | source)
XLA Modules:
  0.0 235.7 jit_solution(1966042756070095992)
XLA Ops:
  0.6 229.0 %layer.1 = (bf16[4,4,128,384]{3,2,1,0:T(8,128)(2,1)}, bf16[4,4,128,384]{3,2,1,0:T(8,128)(2,1)}, bf16[4,4,128,384]{3,2,1,0:T(8,128)(2,1)}, bf16[4,4,128,384]{3,2,1,0:T(8,128)(2,1)}, bf16[4,4,128,384]{3,2,1,0:T(8,128)(2,1)}) custom-call(bf16[8,128,768]{2,1,0:T(8,128)(2,1)} %q_row.1, bf16[8,128,768]{2,1,0:T(8,128)(2,1)} %k_row.1, bf16[8,128,768]{2,1,0:T(8,128)(2,1)} %v_row.1, ...), custom_call_target="tpu_custom_call" | custom-call | tf_op jit(solution)/shard_map/layer/pallas_call | solution.py:602
  229.7 6.0 %unpack.1 = (bf16[2,4,128,768]{3,2,1,0:T(8,128)(2,1)}, bf16[2,4,128,768]{3,2,1,0:T(8,128)(2,1)}, bf16[2,4,128,768]{3,2,1,0:T(8,128)(2,1)}, bf16[2,4,128,768]{3,2,1,0:T(8,128)(2,1)}, bf16[2,4,128,768]{3,2,1,0:T(8,128)(2,1)}) custom-call(bf16[4,4,128,384]{3,2,1,0:T(8,128)(2,1)} %get-tuple-element.15.refs_0_, ...), custom_call_target="tpu_custom_call" | custom-call | tf_op jit(solution)/shard_map/unpack/pallas_call | solution.py:68

commit v5 on v4

--- a/solution.py
+++ b/solution.py
@@ -303,12 +303,10 @@
     load(1).start()
     loop(6, lambda i: greet(dev(x, y, (z + 1 + i // 2) % 4, i % 2)))
     loop(31, lambda i: greet(plane_dest(i + 1)[0]))
-    loop(32, lambda i: greet(col_dest(i)))
-    loop(32, lambda i: greet(col_home(i)[0]))
     pack_next(0)
     pack_next(1)
     pack_next(2)
-    pl.semaphore_wait(barrier, 101 - jnp.where(home_mine, 2, 0))
+    pl.semaphore_wait(barrier, 37)
 
     def send_rows(n, dst):
         def body(i, maybe_me):

time: 236 us -> 235 us (level)
  no operation moved by 1% of the time
where the time goes in v5:
time: 235 us
  Pallas kernels  234 us (100%)
    pallas_call x1, Pallas kernels, on_device(): pl.pallas_call(main_kernel, name='layer', out_shape=[jax.ShapeDtypeStruct...  228 us
    pallas_call x1, Pallas kernels, unpack(): pl.pallas_call(unpack_kernel, name='unpack', grid=(2,), out_shape=[jax.Sh...  6 us

profile of v5, /device:TPU:1, one launch (start us, length us, event | category | flops | bytes accessed | tf_op | source)
XLA Modules:
  0.0 234.6 jit_solution(16640751459588502187)
XLA Ops:
  0.6 227.9 %layer.1 = (bf16[4,4,128,384]{3,2,1,0:T(8,128)(2,1)}, bf16[4,4,128,384]{3,2,1,0:T(8,128)(2,1)}, bf16[4,4,128,384]{3,2,1,0:T(8,128)(2,1)}, bf16[4,4,128,384]{3,2,1,0:T(8,128)(2,1)}, bf16[4,4,128,384]{3,2,1,0:T(8,128)(2,1)}) custom-call(bf16[8,128,768]{2,1,0:T(8,128)(2,1)} %q_row.1, bf16[8,128,768]{2,1,0:T(8,128)(2,1)} %k_row.1, bf16[8,128,768]{2,1,0:T(8,128)(2,1)} %v_row.1, ...), custom_call_target="tpu_custom_call" | custom-call | tf_op jit(solution)/shard_map/layer/pallas_call | solution.py:600
  228.6 6.0 %unpack.1 = (bf16[2,4,128,768]{3,2,1,0:T(8,128)(2,1)}, bf16[2,4,128,768]{3,2,1,0:T(8,128)(2,1)}, bf16[2,4,128,768]{3,2,1,0:T(8,128)(2,1)}, bf16[2,4,128,768]{3,2,1,0:T(8,128)(2,1)}, bf16[2,4,128,768]{3,2,1,0:T(8,128)(2,1)}) custom-call(bf16[4,4,128,384]{3,2,1,0:T(8,128)(2,1)} %get-tuple-element.15.refs_0_, ...), custom_call_target="tpu_custom_call" | custom-call | tf_op jit(solution)/shard_map/unpack/pallas_call | solution.py:68
